TPU v7x, 32 devices: a whole 2x2x4 slice. The times are simulated.
32 devices in a mesh: dp: 8 (over y, x, core), index: 4 (over z).
Axes of the slice: x: 2, y: 2, z: 4, core: 2. Of those that a mesh axis runs over, the one named last changes fastest.
Arguments:
- queries: bfloat16 [4096, 1024], P(('dp', 'index')), may hold values from -0.1875 to 0.1875
- keys: bfloat16 [2048, 1024], P(('dp', 'index')), may hold values from -6 to 6
- pattern: int32 [32, 256], P(('dp', 'index')), may hold values 0 or 1
- clusters: int32 [2048], P(('dp', 'index')), may hold values from 0 to 255
- positives: int32 [4096], P(('dp', 'index')), may hold values from 0 to 2047
- loss_multiplier: float32 [4096], P(('dp', 'index')), may hold values from -4 to 4
Outputs:
- query_grad: float32 [4096, 1024], P(('dp', 'index'))
- loss: float32 [4096], P(('dp', 'index'))
All inputs are finite; a program needn't handle non-finite values. No bound on the sum of `pattern` on one device may be relied on, other than what follows from the above.
Results may differ from a plain program's by a relative error of at most 0.0029.
Values may be sent and summed in bfloat16 or wider, within the bound.
No kernel may reach another device: no remote copies, remote signals or barrier semaphores. Data moves between devices by JAX's collectives and lax.ppermute only.
A program may use at most 64 MiB of HBM per device.

v0:
```python
import jax
import jax.numpy as jnp
from jax import lax
from jax.sharding import PartitionSpec as P

logit_divisor = 0.1
epsilon = 1e-06


def shifted(value, axis, steps):
    count = lax.axis_size(axis)
    pairs = [(source, (source + steps) % count) for source in range(count)]
    return lax.ppermute(value, axis, pairs)


def unit_rows(values):
    floats = values.astype(jnp.float32)
    scaling = lax.rsqrt(jnp.sum(floats * floats, axis=1, keepdims=True) + epsilon)
    return (floats, scaling)


def tile_weights(key_tile, cluster_tile, first_key, gathered, pattern_rows, positive_indices):
    inner_product_matrix = (
        lax.dot_general(
            key_tile, gathered, (((1,), (1,)), ((), ())), preferred_element_type=jnp.float32
        )
        / logit_divisor
    )
    cluster_ids = cluster_tile.astype(jnp.int32)
    onehot = (
        cluster_ids[:, None] == jnp.arange(pattern_rows.shape[1], dtype=jnp.int32)[None, :]
    ).astype(jnp.float32)
    allowed = lax.dot_general(
        onehot, pattern_rows, (((1,), (1,)), ((), ())), precision=lax.Precision.HIGHEST
    )
    allowed = jnp.repeat(allowed, gathered.shape[0] // pattern_rows.shape[0], axis=1)
    key_ids = first_key + jnp.arange(key_tile.shape[0], dtype=jnp.int32)
    is_positive = (key_ids[:, None] == positive_indices[None, :]).astype(jnp.float32)
    weights = jnp.exp(inner_product_matrix) * jnp.maximum(allowed, is_positive)
    return (weights, jnp.sum(weights, axis=0), jnp.sum(inner_product_matrix * is_positive, axis=0))


def body(queries, keys, pattern, clusters, positives, loss_multiplier):
    query_floats, query_scale = unit_rows(queries)
    query_norm = (query_floats * query_scale).astype(jnp.bfloat16)
    key_floats, key_scale = unit_rows(keys)
    passage_magnitude = (key_floats * key_scale).astype(jnp.bfloat16)
    cluster_wire = clusters.astype(jnp.bfloat16)
    id_pair = jnp.stack([positives // 256, positives % 256], axis=1).astype(jnp.bfloat16)
    gathered, pattern_low, pair_rows = (
        lax.all_gather(query_norm, "dp", axis=0, tiled=True),
        lax.all_gather(pattern.astype(jnp.bfloat16), "dp", axis=0, tiled=True),
        lax.all_gather(id_pair, "dp", axis=0, tiled=True),
    )
    pattern_rows = pattern_low.astype(jnp.float32)
    pair_floats = pair_rows.astype(jnp.float32)
    positive_indices = (pair_floats[:, 0] * 256.0 + pair_floats[:, 1]).astype(jnp.int32)
    cycle_size = lax.axis_size("index")
    row_index = lax.axis_index("dp")
    col_index = lax.axis_index("index")
    tile_rows = keys.shape[0]
    total_rows = gathered.shape[0]
    row_base = row_index * cycle_size
    key_store = jnp.zeros((cycle_size, tile_rows, keys.shape[1]), jnp.bfloat16)
    weight_store = jnp.zeros((cycle_size, tile_rows, total_rows), jnp.bfloat16)
    carried = (
        key_store,
        weight_store,
        jnp.zeros((total_rows,), jnp.float32),
        jnp.zeros((total_rows,), jnp.float32),
    )

    def absorb(carried, slot_index, key_tile, cluster_tile, first_key, row_offset):
        key_store, weight_store, sums, positive_scores = carried
        weights, part_sums, part_scores = tile_weights(
            key_tile, cluster_tile, first_key, gathered, pattern_rows, positive_indices
        )
        offset_row = jnp.int32(row_offset)
        key_store = lax.dynamic_update_slice(
            key_store, key_tile[None], (slot_index, offset_row, jnp.int32(0))
        )
        weight_store = lax.dynamic_update_slice(
            weight_store, weights.astype(jnp.bfloat16)[None], (slot_index, offset_row, jnp.int32(0))
        )
        return (key_store, weight_store, sums + part_sums, positive_scores + part_scores)

    row_start = row_base * tile_rows
    offsets = positive_indices - row_start
    in_row = (offsets >= 0) & (offsets < cycle_size * tile_rows)
    safe_offsets = jnp.clip(offsets, 0, cycle_size * tile_rows - 1)
    source_ids = safe_offsets // tile_rows
    within = safe_offsets % tile_rows

    def cycle_turn(cycle_step, cycle_carry):
        carried, key_tile, cluster_tile = cycle_carry
        source = (col_index - cycle_step) % cycle_size
        carried = absorb(
            carried, cycle_step, key_tile, cluster_tile, (row_base + source) * tile_rows, 0
        )
        key_tile, cluster_tile = shifted((key_tile, cluster_tile), "index", 1)
        return (carried, key_tile, cluster_tile)

    carried, key_tile, cluster_tile = lax.fori_loop(
        0, cycle_size - 1, cycle_turn, (carried, passage_magnitude, cluster_wire)
    )
    last_step = jnp.int32(cycle_size - 1)
    source = (col_index - last_step) % cycle_size
    carried = absorb(carried, last_step, key_tile, cluster_tile, (row_base + source) * tile_rows, 0)
    slots = (col_index - source_ids) % cycle_size
    key_store, weight_store, sums, positive_scores = carried
    expected = lax.dot_general(
        weight_store, key_store, (((0, 1), (0, 1)), ((), ())), preferred_element_type=jnp.float32
    )
    flat_keys = key_store.reshape(cycle_size * tile_rows, key_store.shape[2])
    picked = flat_keys[slots * tile_rows + within]
    selected_lower = jnp.where(in_row[:, None], picked, jnp.zeros_like(picked))
    mine_expected, mine_positive, mine_sums, mine_scores = (
        lax.psum_scatter(expected, "dp", scatter_dimension=0, tiled=True),
        lax.psum_scatter(selected_lower.astype(jnp.float32), "dp", scatter_dimension=0, tiled=True),
        lax.psum_scatter(sums, "dp", scatter_dimension=0, tiled=True),
        lax.psum_scatter(positive_scores, "dp", scatter_dimension=0, tiled=True),
    )
    update_direction_entry = mine_expected / mine_sums[:, None] - mine_positive
    question_derivative = update_direction_entry * (loss_multiplier / logit_divisor)[:, None]
    projection = jnp.sum(query_floats * question_derivative, axis=1, keepdims=True)
    query_grad = (
        query_scale * question_derivative
        - query_scale * query_scale * query_scale * query_floats * projection
    )
    loss_values = jnp.log(mine_sums) - mine_scores
    return (query_grad, loss_values)


def solution(mesh):
    in_specs = (
        P(("dp", "index"), None),
        P(("dp", "index"), None),
        P(("dp", "index"), None),
        P(("dp", "index")),
        P(("dp", "index")),
        P(("dp", "index")),
    )
    out_specs = (P(("dp", "index"), None), P(("dp", "index")))
    return jax.shard_map(body, mesh=mesh, in_specs=in_specs, out_specs=out_specs, check_vma=False)
```

profile of v0, /device:TPU:0, one launch (start us, length us, event | category | flops | bytes accessed | tf_op | source)
XLA Modules:
  0.0 182.1 jit_solution(3897848392268209464)
XLA Ops:
  7.2 1.1 fusion.6
  8.3 1.8 fusion.7
  10.2 0.7 convert_bitcast_fusion.1
  10.9 10.2 %all_gather.11 = bf16[1024,2]{0,1:T(2,128)(2,1)S(1)} all-gather(bf16[128,2]{0,1:T(2,128)(2,1)S(1)} %pad_maximum_fusion), channel_id=1, replica_groups=mesh['dp'=8,'index'=4] {'dp'}, dimensions={0}, use_global_device_ids=true | all-gather | bytes 4608 | tf_op jit(solution)/shard_map/all_gather | solution.py:53
  21.1 0.7 convert_element_type.86
  21.7 0.7 convert_bitcast_fusion
  22.4 8.9 %all-gather = bf16[8,1,256]{2,1,0:T(2,128)(2,1)S(1)} all-gather(bf16[1,1,256]{2,1,0:T(2,128)(2,1)S(1)} %convert_bitcast_fusion), channel_id=1, replica_groups=mesh['dp'=8,'index'=4] {'dp'}, dimensions={0}, use_global_device_ids=true | all-gather | bytes 4608 | tf_op jit(solution)/shard_map/all_gather | solution.py:52
  31.3 1.1 fusion.11
  32.4 1.0 fusion.12
  33.4 7.7 %all-gather.3.cloned.1.call-done = bf16[1024,1024]{1,0:T(8,128)(2,1)} async-done(((bf16[128,1024]{1,0:T(8,128)(2,1)}), bf16[1024,1024]{1,0:T(8,128)(2,1)}) %all-gather.3.cloned.1.call-update) | async-done | bytes 2097168 | tf_op jit(solution)/shard_map/all_gather | solution.py:51
  41.2 21.4 %while.26 = (s32[]{:T(128)}, bf16[4,64,1024]{2,1,0:T(8,128)(2,1)S(1)}, bf16[4,64,1024]{2,1,0:T(8,128)(2,1)S(1)}, f32[1024]{0:T(1024)S(1)}, f32[1024]{0:T(1024)S(...) while((s32[]{:T(128)}, ...), condition=%wide.region_5.6_spmd.clone, body=%wide.region_2.5_spmd.clone.sunk | while | flops 136661136 | bytes 4774676 | solution.py:103
  41.2 1.5 collective-permute-start
  42.8 1.5 collective-permute-start.1
  44.6 2.4 %bitcast_dynamic-update-slice_fusion.7 = (bf16[4,64,1024]{2,1,0:T(8,128)(2,1)S(1)}, f32[64,1024]{1,0:T(8,128)S(1)}) fusion(bf16[4,64,1024]{2,1,0:T(8,128)(2,1)S(1)} %get-tuple-element.487, s32[]{:T(128)} %get-tuple-element.485, s32[1024]{0:T(1024)S(1)} %get-tuple-element.513, s32[64]{0:T(128)S(1)} %iota_add_fusion.3, ...), kind=kOutput, calls=%fused_computation.7.clone.1 | convolution fusion | flops 134610944 | bytes 2888196 | tf_op jit(solution)/shard_map/while/body/eval_jaxpr/dot_general | solution.py:24
  47.2 1.6 collective-permute-done.1
  48.9 1.2 collective-permute-start.1
  50.4 2.4 %bitcast_dynamic-update-slice_fusion.7 = (bf16[4,64,1024]{2,1,0:T(8,128)(2,1)S(1)}, f32[64,1024]{1,0:T(8,128)S(1)}) fusion(bf16[4,64,1024]{2,1,0:T(8,128)(2,1)S(1)} %get-tuple-element.487, s32[]{:T(128)} %get-tuple-element.485, s32[1024]{0:T(1024)S(1)} %get-tuple-element.513, s32[64]{0:T(128)S(1)} %iota_add_fusion.3, ...), kind=kOutput, calls=%fused_computation.7.clone.1 | convolution fusion | flops 134610944 | bytes 2888196 | tf_op jit(solution)/shard_map/while/body/eval_jaxpr/dot_general | solution.py:24
  53.0 2.7 %collective-permute-done.1 = bf16[64]{0:T(256)(128)(2,1)S(1)} collective-permute-done((bf16[64]{0:T(256)(128)(2,1)S(1)}, bf16[64]{0:T(256)(128)(2,1)S(1)}, u32[]{:S(2)}, u32[]{:S(2)}) %collective-permute-start.1) | collective-permute-done | bytes 160 | tf_op jit(solution)/shard_map/while/body/eval_jaxpr/ppermute | solution.py:13
  55.8 1.1 collective-permute-start.1
  57.3 2.4 %bitcast_dynamic-update-slice_fusion.7 = (bf16[4,64,1024]{2,1,0:T(8,128)(2,1)S(1)}, f32[64,1024]{1,0:T(8,128)S(1)}) fusion(bf16[4,64,1024]{2,1,0:T(8,128)(2,1)S(1)} %get-tuple-element.487, s32[]{:T(128)} %get-tuple-element.485, s32[1024]{0:T(1024)S(1)} %get-tuple-element.513, s32[64]{0:T(128)S(1)} %iota_add_fusion.3, ...), kind=kOutput, calls=%fused_computation.7.clone.1 | convolution fusion | flops 134610944 | bytes 2888196 | tf_op jit(solution)/shard_map/while/body/eval_jaxpr/dot_general | solution.py:24
  59.9 2.7 %collective-permute-done.1 = bf16[64]{0:T(256)(128)(2,1)S(1)} collective-permute-done((bf16[64]{0:T(256)(128)(2,1)S(1)}, bf16[64]{0:T(256)(128)(2,1)S(1)}, u32[]{:S(2)}, u32[]{:S(2)}) %collective-permute-start.1) | collective-permute-done | bytes 160 | tf_op jit(solution)/shard_map/while/body/eval_jaxpr/ppermute | solution.py:13
  63.0 2.4 %bitcast_dynamic-update-slice_fusion.3 = (bf16[4,64,1024]{2,1,0:T(8,128)(2,1)S(1)}, f32[64,1024]{1,0:T(8,128)S(1)}) fusion(bf16[4,64,1024]{2,1,0:T(8,128)(2,1)S(1)} %get-tuple-element.294, s32[1024]{0:T(1024)S(1)} %get-tuple-element.534, s32[64]{0:T(128)S(1)} %iota_add_fusion.1, f32[8,8,8,128]{3,2,1,0:T(8,128)S(1)} %bitcast.62, ...), kind=kOutput, calls=%fused_computation.39 | convolution fusion | flops 134610944 | bytes 2888192 | tf_op jit(solution)/shard_map/dot_general | solution.py:24
  65.3 2.7 %convolution_bitcast_fusion = f32[1024,1024]{1,0:T(8,128)} fusion(bf16[4,64,1024]{2,1,0:T(8,128)(2,1)S(1)} %get-tuple-element.381, bf16[4,64,1024]{2,1,0:T(8,128)(2,1)S(1)} %bitcast_dynamic-update-slice_fusion.2), kind=kOutput, calls=%fused_computation.16 | convolution fusion | flops 536870912 | bytes 5242880 | tf_op jit(solution)/shard_map/dot_general | solution.py:111
  68.2 4.1 %gather_fusion = bf16[1024,1024]{1,0:T(8,128)(2,1)S(1)} fusion(bf16[256,1024]{1,0:T(8,128)(2,1)S(1)} %bitcast.59, s32[1024]{0:T(1024)S(1)} %broadcast_clamp_fusion), kind=kCustom, calls=%fused_computation | custom fusion | bytes 4198400 | tf_op jit(solution)/shard_map/gather | solution.py:115
  72.3 2.3 %select_convert_fusion = f32[1024,1024]{1,0:T(8,128)} fusion(bf16[1024,1024]{1,0:T(8,128)(2,1)S(1)} %gather_fusion, pred[1024]{0:T(1024)(128)(4,1)S(1)} %get-tuple-element.369), kind=kLoop, calls=%fused_computation.17 | loop fusion | flops 2097152 | bytes 6292480 | tf_op jit(solution)/shard_map/convert_element_type | solution.py:119
  74.6 0.6 copy-done.2
  76.7 12.1 %all-reduce.2 = (f32[1024]{0:T(1024)S(1)}, f32[1024]{0:T(1024)S(1)}) all-reduce(f32[1024]{0:T(1024)S(1)} %add.194, f32[1024]{0:T(1024)S(1)} %add.199), channel_id=3, replica_groups=mesh['dp'=8,'index'=4] {'dp'}, use_global_device_ids=true, to_apply=%region_8.9.clone | all-reduce | flops 2048 | bytes 16384
  88.8 0.6 dynamic-slice_subtract_fusion
  89.4 27.3 %reduce-scatter.3.cloned.1.call-done = f32[128,1024]{1,0:T(8,128)} async-done(((f32[1024,1024]{1,0:T(8,128)}), f32[128,1024]{1,0:T(8,128)}) %reduce-scatter.3.cloned.1.call-update) | async-done | bytes 524304 | tf_op jit(solution)/shard_map/reduce_scatter | solution.py:118
  116.8 55.1 %reduce-scatter.5.cloned.1.call-done = f32[128,1024]{1,0:T(8,128)} async-done(((f32[1024,1024]{1,0:T(8,128)}), f32[128,1024]{1,0:T(8,128)}) %reduce-scatter.5.cloned.1.call-update) | async-done | bytes 524304 | tf_op jit(solution)/shard_map/reduce_scatter | solution.py:119
  171.9 1.5 fusion.10
  173.4 2.2 %fusion.9 = f32[128,1024]{1,0:T(8,128)} fusion(bf16[128,1024]{1,0:T(8,128)(2,1)S(1)} %copy-done, f32[128]{0:T(128)S(1)} %fusion.10, f32[128]{0:T(128)S(1)} %get-tuple-element.377, f32[128]{0:T(128)S(1)} %get-tuple-element.378, f32[128]{0:T(128)S(1)} %broadcast_multiply_fusion, f32[128,1024]{1,0:T(8,128)} %reduce-scatter.5.cloned.1.call-done, ...), kind=kLoop, calls=%fused_computation.26 | loop fusion | flops 1048576 | bytes 1837568 | tf_op jit(solution)/shard_map/sub | solution.py:127
  (65 shorter events, 3.4 us)
Async XLA Ops:
  7.2 33.9 %all-gather.3.cloned.1.call-start = ((), (), s32[]{:S(2)}) async-start(), calls=%async_computation.2 | async-start | bytes 2359296 | tf_op jit(solution)/shard_map/all_gather | solution.py:51
  10.1 106.7 %reduce-scatter.3.cloned.1.call-start = ((), (), s32[]{:S(2)}) async-start(), calls=%async_computation.3 | async-start | bytes 4718592 | tf_op jit(solution)/shard_map/reduce_scatter | solution.py:118
  41.2 7.6 %collective-permute-start = (bf16[64,1024]{1,0:T(8,128)(2,1)S(1)}, bf16[64,1024]{1,0:T(8,128)(2,1)S(1)}, u32[]{:S(2)}, u32[]{:S(2)}) collective-permute-start(bf16[64,1024]{1,0:T(8,128)(2,1)S(1)} %copy.50), channel_id=1, source_target_pairs={{0,1},{1,2},{2,3},{3,0},{4,5},{5,6},{6,7},{7,4},{8,9},{9,10},{10,1... | collective-permute-start | bytes 393224 | tf_op jit(solution)/shard_map/while/body/eval_jaxpr/ppermute | solution.py:13
  42.8 6.0 %collective-permute-start.1 = (bf16[64]{0:T(256)(128)(2,1)S(1)}, bf16[64]{0:T(256)(128)(2,1)S(1)}, u32[]{:S(2)}, u32[]{:S(2)}) collective-permute-start(bf16[64]{0:T(256)(128)(2,1)S(1)} %copy.51), channel_id=1, source_target_pairs={{0,1},{1,2},{2,3},{3,0},{4,5},{5,6},{6,7},{7,4},{8,9},{9,10},{10,1... | collective-permute-start | bytes 392 | tf_op jit(solution)/shard_map/while/body/eval_jaxpr/ppermute | solution.py:13
  48.8 6.9 %collective-permute-start = (bf16[64,1024]{1,0:T(8,128)(2,1)S(1)}, bf16[64,1024]{1,0:T(8,128)(2,1)S(1)}, u32[]{:S(2)}, u32[]{:S(2)}) collective-permute-start(bf16[64,1024]{1,0:T(8,128)(2,1)S(1)} %copy.50), channel_id=1, source_target_pairs={{0,1},{1,2},{2,3},{3,0},{4,5},{5,6},{6,7},{7,4},{8,9},{9,10},{10,1... | collective-permute-start | bytes 393224 | tf_op jit(solution)/shard_map/while/body/eval_jaxpr/ppermute | solution.py:13
  48.9 6.8 %collective-permute-start.1 = (bf16[64]{0:T(256)(128)(2,1)S(1)}, bf16[64]{0:T(256)(128)(2,1)S(1)}, u32[]{:S(2)}, u32[]{:S(2)}) collective-permute-start(bf16[64]{0:T(256)(128)(2,1)S(1)} %copy.51), channel_id=1, source_target_pairs={{0,1},{1,2},{2,3},{3,0},{4,5},{5,6},{6,7},{7,4},{8,9},{9,10},{10,1... | collective-permute-start | bytes 392 | tf_op jit(solution)/shard_map/while/body/eval_jaxpr/ppermute | solution.py:13
  55.7 6.9 %collective-permute-start = (bf16[64,1024]{1,0:T(8,128)(2,1)S(1)}, bf16[64,1024]{1,0:T(8,128)(2,1)S(1)}, u32[]{:S(2)}, u32[]{:S(2)}) collective-permute-start(bf16[64,1024]{1,0:T(8,128)(2,1)S(1)} %copy.50), channel_id=1, source_target_pairs={{0,1},{1,2},{2,3},{3,0},{4,5},{5,6},{6,7},{7,4},{8,9},{9,10},{10,1... | collective-permute-start | bytes 393224 | tf_op jit(solution)/shard_map/while/body/eval_jaxpr/ppermute | solution.py:13
  55.8 6.8 %collective-permute-start.1 = (bf16[64]{0:T(256)(128)(2,1)S(1)}, bf16[64]{0:T(256)(128)(2,1)S(1)}, u32[]{:S(2)}, u32[]{:S(2)}) collective-permute-start(bf16[64]{0:T(256)(128)(2,1)S(1)} %copy.51), channel_id=1, source_target_pairs={{0,1},{1,2},{2,3},{3,0},{4,5},{5,6},{6,7},{7,4},{8,9},{9,10},{10,1... | collective-permute-start | bytes 392 | tf_op jit(solution)/shard_map/while/body/eval_jaxpr/ppermute | solution.py:13
  68.0 103.9 %reduce-scatter.5.cloned.1.call-start = ((), (), s32[]{:S(2)}) async-start(), calls=%async_computation.4 | async-start | bytes 4718592 | tf_op jit(solution)/shard_map/reduce_scatter | solution.py:119
  74.6 0.7 copy-start.2
  74.6 1.9 %copy-start.1 = (f32[128]{0:T(128)S(1)}, f32[128]{0:T(128)}, u32[]{:S(2)}) copy-start(f32[128]{0:T(128)} %param.13) | copy-start | bytes 1540
  74.6 97.3 %copy-start = (bf16[128,1024]{1,0:T(8,128)(2,1)S(1)}, bf16[128,1024]{1,0:T(8,128)(2,1)}, u32[]{:S(2)}) copy-start(bf16[128,1024]{1,0:T(8,128)(2,1)} %param.8) | copy-start | bytes 786436
Sparse Core Ops, SparseCore 0:
  10.5 30.5 all-gather.2
  68.2 48.5 reduce-scatter.2
  120.5 51.3 reduce-scatter.4
where the time goes:
time: 183 us; the launch traced here: 182 us
  waiting for transfers between devices  97.1 us (53%)
  blocking collectives  31.2 us (17%)
  between operations  14.6 us (8%)
  other arithmetic  14.4 us (8%)
  matrix products  13 us (7%)
  local copies, waits for them, and re-layouts  5.99 us (3%)
  starting transfers between devices  5.53 us (3%)
    reduce_scatter x1, waiting for transfers between devices, body(): lax.psum_scatter(selected_lower.astype(jnp.float32), 'dp', scatter_dimens...  55.1 us
    reduce_scatter x1, waiting for transfers between devices, body(): lax.psum_scatter(expected, 'dp', scatter_dimension=0, tiled=True)  27.3 us
    unnamed x1, blocking collectives  12.1 us
    all_gather x1, blocking collectives, body(): lax.all_gather(id_pair, 'dp', axis=0, tiled=True)  10.2 us
    dot_general x4, matrix products, tile_weights(): lax.dot_general(key_tile, gathered, (((1,), (1,)), ((), ())), preferred_e...  9.5 us
    all_gather x1, blocking collectives, body(): lax.all_gather(pattern.astype(jnp.bfloat16), 'dp', axis=0, tiled=True)  8.86 us
    all_gather x1, waiting for transfers between devices, body(): lax.all_gather(query_norm, 'dp', axis=0, tiled=True)  7.66 us
    ppermute x6, waiting for transfers between devices, shifted(): return lax.ppermute(value, axis, pairs)  6.96 us
  transfers between devices with their start and end apart: 9, of which 6 were waited for; matrix products, arithmetic and copies ran while one was open for 11% of the time, Pallas kernels for 0%

commit v1 on v0

v1 whole, which is shorter than its diff:
```python
import functools

import jax
import jax.numpy as jnp
from jax import lax
from jax.experimental import pallas as pl
from jax.experimental.pallas import tpu as pltpu
from jax.sharding import PartitionSpec as P

logit_divisor = 0.1
epsilon = 1e-06
AXES = ("dp", "index")
LANES = 128
TAG_ROWS = 16
VMEM = pl.BlockSpec(memory_space=pltpu.VMEM)


def exchange(value, counts, flip):
    total = counts[0] * counts[1]
    return lax.ppermute(value, AXES, [(i, flip(i)) for i in range(total)])


def pack_kernel(keys_ref, clusters_ref, wire_ref):
    rows, width = keys_ref.shape
    floats = keys_ref[...].astype(jnp.float32)
    scale = lax.rsqrt(jnp.sum(floats * floats, axis=1, keepdims=True) + epsilon)
    unit = (floats * scale).astype(jnp.bfloat16)
    tiles = width // LANES
    for t in range(tiles):
        wire_ref[t * rows : (t + 1) * rows, :] = unit[:, t * LANES : (t + 1) * LANES]
    device = lax.axis_index("dp") * lax.axis_size("index") + lax.axis_index("index")
    place = lax.broadcasted_iota(jnp.int32, (TAG_ROWS, LANES), 1) % rows
    line = lax.broadcasted_iota(jnp.int32, (TAG_ROWS, LANES), 0)
    key_id = device * rows + place
    clusters = clusters_ref[...].reshape(1, rows)
    clusters = jnp.concatenate([clusters] * (LANES // rows), axis=1)
    tag = jnp.where(line == 0, clusters, jnp.where(line == 1, key_id // 256, key_id % 256))
    wire_ref[tiles * rows :, :] = tag.astype(jnp.float32).astype(jnp.bfloat16)


def pack(keys, clusters):
    rows, width = keys.shape
    return pl.pallas_call(
        pack_kernel,
        out_shape=jax.ShapeDtypeStruct((width // LANES * rows + TAG_ROWS, LANES), jnp.bfloat16),
        in_specs=[VMEM, VMEM],
        out_specs=VMEM,
        name="pack",
    )(keys, clusters)


def main_kernel(rows, group, queries_ref, pattern_ref, positives_ref, multiplier_ref, *refs):
    wires, (grad_ref, loss_ref, key_ref) = refs[:-3], refs[-3:]
    count, width = queries_ref.shape
    tiles = width // LANES
    per = LANES // rows
    wire_rows = tiles * rows + TAG_ROWS
    shards = [(wire, n * wire_rows) for wire in wires for n in range(wire.shape[0] // wire_rows)]
    lane = lax.broadcasted_iota(jnp.int32, (1, LANES), 1)
    diagonal = lax.broadcasted_iota(jnp.int32, (count, count), 0) == lax.broadcasted_iota(
        jnp.int32, (count, count), 1
    )

    def as_column(row):
        return jnp.sum(jnp.where(diagonal, row, 0.0), axis=1, keepdims=True)

    floats = queries_ref[...].astype(jnp.float32)
    scale = lax.rsqrt(jnp.sum(floats * floats, axis=1, keepdims=True) + epsilon)
    unit = (floats * scale).astype(jnp.bfloat16)
    positive = as_column(positives_ref[...].reshape(1, count).astype(jnp.float32))
    multiplier = as_column(multiplier_ref[...].reshape(1, count))
    clusters_all = pattern_ref.shape[1]
    marks = jnp.broadcast_to(
        pattern_ref[...].astype(jnp.float32).astype(jnp.bfloat16), (16, clusters_all)
    )

    def absorb(some):
        cluster_parts, id_parts = [], []
        for first in range(0, len(some), per):
            tag = None
            for j in range(per):
                wire, base = some[first + j]
                slot = (first + j) * rows
                for t in range(tiles):
                    key_ref[slot : slot + rows, t * LANES : (t + 1) * LANES] = wire[
                        base + t * rows : base + (t + 1) * rows, :
                    ]
                mine = wire[base + tiles * rows : base + wire_rows, :].astype(jnp.float32)
                tag = mine if tag is None else jnp.where(lane >= j * rows, mine, tag)
            cluster_parts.append(tag[0:1, :])
            id_parts.append(tag[1:2, :] * 256.0 + tag[2:3, :])
        cluster_row = jnp.concatenate(cluster_parts, axis=1)
        id_row = jnp.concatenate(id_parts, axis=1)
        keys = key_ref[: len(some) * rows, :]
        scores = (
            lax.dot_general(unit, keys, (((1,), (1,)), ((), ())), preferred_element_type=jnp.float32)
            / logit_divisor
        )
        onehot = (
            lax.broadcasted_iota(jnp.int32, (clusters_all, 1), 0).astype(jnp.float32) == cluster_row
        )
        allowed = lax.dot_general(
            marks,
            onehot.astype(jnp.float32).astype(jnp.bfloat16),
            (((1,), (0,)), ((), ())),
            preferred_element_type=jnp.float32,
        )[0:1, :]
        is_positive = (positive == id_row).astype(jnp.float32)
        weights = jnp.exp(scores) * jnp.maximum(allowed, is_positive)
        both = jnp.concatenate(
            [weights.astype(jnp.bfloat16), is_positive.astype(jnp.bfloat16)], axis=0
        )
        return (
            jnp.sum(weights, axis=1, keepdims=True),
            jnp.sum(scores * is_positive, axis=1, keepdims=True),
            lax.dot_general(both, keys, (((1,), (0,)), ((), ())), preferred_element_type=jnp.float32),
        )

    parts = [absorb(shards[first : first + group]) for first in range(0, len(shards), group)]
    totals, positive_score, sums = (functools.reduce(jnp.add, column) for column in zip(*parts))
    direction = sums[:count] / totals - sums[count:]
    gradient = direction * (multiplier / logit_divisor)
    projection = jnp.sum(floats * gradient, axis=1, keepdims=True)
    grad_ref[...] = scale * gradient - scale * scale * scale * floats * projection
    loss = jnp.log(totals) - positive_score
    loss_ref[...] = jnp.sum(jnp.where(diagonal, loss, 0.0), axis=0, keepdims=True).reshape(count)


def finish(rows, queries, pattern, positives, multiplier, wires):
    count, width = queries.shape
    wire_rows = width // LANES * rows + TAG_ROWS
    group = min(32, sum(wire.shape[0] // wire_rows for wire in wires))
    return pl.pallas_call(
        functools.partial(main_kernel, rows, group),
        out_shape=(
            jax.ShapeDtypeStruct((count, width), jnp.float32),
            jax.ShapeDtypeStruct((count,), jnp.float32),
        ),
        in_specs=[VMEM] * (4 + len(wires)),
        out_specs=(VMEM, VMEM),
        scratch_shapes=[pltpu.VMEM((group * rows, width), jnp.bfloat16)],
        compiler_params=pltpu.CompilerParams(vmem_limit_bytes=56 * 1024 * 1024),
        name="finish",
    )(queries, pattern, positives, multiplier, *wires)


def body(counts, queries, keys, pattern, clusters, positives, loss_multiplier):
    dp, index = counts
    rows = keys.shape[0]
    index_bits = index.bit_length() - 1
    dp_bits = dp.bit_length() - 1
    core = index_bits
    plane = list(range(index_bits + 1, index_bits + dp_bits))

    def along(value, bit):
        return exchange(value, counts, lambda i: i ^ (1 << bit))

    def along_plane(value, step):
        first, second = plane[step], plane[len(plane) - 1 - step]
        return exchange(
            value, counts, lambda i: i ^ (1 << (second if (i >> core) & 1 else first))
        )

    column = [pack(keys, clusters)]
    for bit in reversed(range(index_bits)):
        column += [along(value, bit) for value in column]
    if len(column) > 4:
        column = [jnp.concatenate(column, axis=0)]
    held = []
    for value in column:
        block = [value]
        for step in range(len(plane)):
            block += [along_plane(item, step) for item in block]
        held += block + [along(item, core) for item in block]
    return finish(rows, queries, pattern, positives, loss_multiplier, held)


def solution(mesh):
    counts = (mesh.shape["dp"], mesh.shape["index"])
    in_specs = (
        P(AXES, None),
        P(AXES, None),
        P(AXES, None),
        P(AXES),
        P(AXES),
        P(AXES),
    )
    out_specs = (P(AXES, None), P(AXES))
    return jax.shard_map(
        functools.partial(body, counts),
        mesh=mesh,
        in_specs=in_specs,
        out_specs=out_specs,
        check_vma=False,
    )
```

time: 183 us -> 47.5 us (0.26)
  waiting for transfers between devices: 97.1 us -> 15.3 us
  blocking collectives: 31.2 us -> 0 us
  starting transfers between devices: 5.53 us -> 22.3 us
  other arithmetic: 14.4 us -> 0 us
  between operations: 14.6 us -> 1.01 us
  matrix products: 13 us -> 0 us
  Pallas kernels: 0 us -> 8.01 us
  local copies, waits for them, and re-layouts: 5.99 us -> 0.77 us
    reduce_scatter x2 -> x0, waiting for transfers between devices: 82.5 us -> none  [the longest x1 55.1 us: body(): lax.psum_scatter(selected_lower.astype(jnp.float32), 'dp', scatter_dimens...]
    all_gather x2 -> x0, blocking collectives: 19.1 us -> none  [the longest x1 10.2 us: body(): lax.all_gather(id_pair, 'dp', axis=0, tiled=True)]
    ppermute x6 -> x31, starting transfers between devices: 5.41 us -> 22.3 us  [exchange(): return lax.ppermute(value, AXES, [(i, flip(i)) for i in range(total)])]
    dot_general x9 -> x0, matrix products: 13 us -> none  [the longest x4 9.5 us: tile_weights(): lax.dot_general(key_tile, gathered, (((1,), (1,)), ((), ())), preferred_e...]
    unnamed x1 -> x0, blocking collectives: 12.1 us -> none
    ppermute x6 -> x31, waiting for transfers between devices: 6.96 us -> 15.3 us  [exchange(): return lax.ppermute(value, AXES, [(i, flip(i)) for i in range(total)])]
    pallas_call x0 -> x2, Pallas kernels: none -> 8.01 us  [the longest x1 6.33 us: finish(): pl.pallas_call(functools.partial(main_kernel, rows, group), out_shape=(ja...]
    all_gather x1 -> x0, waiting for transfers between devices: 7.66 us -> none  [body(): lax.all_gather(query_norm, 'dp', axis=0, tiled=True)]
  transfers between devices with their start and end apart: 9 -> 31, of which waited for: 6 -> 11; matrix products, arithmetic and copies ran while one was open for 11% -> 0% of each run, Pallas kernels for 0% -> 0%
where the time goes in v1:
time: 47.5 us; the launch traced here: 47.3 us
  starting transfers between devices  22.3 us (47%)
  waiting for transfers between devices  15.3 us (32%)
  Pallas kernels  8.01 us (17%)
  between operations  1.01 us (2%)
  local copies, waits for them, and re-layouts  0.77 us (2%)
    ppermute x31, starting transfers between devices, exchange(): return lax.ppermute(value, AXES, [(i, flip(i)) for i in range(total)])  22.3 us
    ppermute x31, waiting for transfers between devices, exchange(): return lax.ppermute(value, AXES, [(i, flip(i)) for i in range(total)])  15.3 us
    pallas_call x1, Pallas kernels, finish(): pl.pallas_call(functools.partial(main_kernel, rows, group), out_shape=(ja...  6.33 us
    pallas_call x1, Pallas kernels, pack(): pl.pallas_call(pack_kernel, out_shape=jax.ShapeDtypeStruct((width // LANE...  1.68 us
  transfers between devices with their start and end apart: 31, of which 11 were waited for; matrix products, arithmetic and copies ran while one was open for 0% of the time, Pallas kernels for 0%

profile of v1, /device:TPU:0, one launch (start us, length us, event | category | flops | bytes accessed | tf_op | source)
XLA Modules:
  0.0 47.3 jit_solution(16460595912084755165)
XLA Ops:
  0.6 1.7 %pack.1.refs_0_ = bf16[528,128]{1,0:T(8,128)(2,1)} custom-call(bf16[64,1024]{1,0:T(8,128)(2,1)} %keys_ref.1, s32[64]{0:T(128)} %clusters_ref.1), custom_call_target="tpu_custom_call" | custom-call | tf_op jit(solution)/shard_map/pack/pallas_call | solution.py:43
  2.3 3.0 %collective-permute-start.15 = (bf16[528,128]{1,0:T(8,128)(2,1)}, bf16[528,128]{1,0:T(8,128)(2,1)S(1)}, u32[]{:S(2)}, u32[]{:S(2)}) collective-permute-start(bf16[528,128]{1,0:T(8,128)(2,1)} %pack.1.refs_0_), channel_id=1, source_target_pairs={{0,1},{1,0},{2,3},{3,2},{4,5},{5,4},{6,7},{7,6},{8,9},{9,8},{10,11... | collective-permute-start | bytes 405512 | tf_op jit(solution)/shard_map/ppermute | solution.py:20
  5.3 2.6 %collective-permute-start.7 = (bf16[528,128]{1,0:T(8,128)(2,1)}, bf16[528,128]{1,0:T(8,128)(2,1)S(1)}, u32[]{:S(2)}, u32[]{:S(2)}) collective-permute-start(bf16[528,128]{1,0:T(8,128)(2,1)} %pack.1.refs_0_), channel_id=1, source_target_pairs={{0,2},{1,3},{2,0},{3,1},{4,6},{5,7},{6,4},{7,5},{8,10},{9,11},{10,... | collective-permute-start | bytes 405512 | tf_op jit(solution)/shard_map/ppermute | solution.py:20
  7.9 1.5 %collective-permute-start.1 = (bf16[528,128]{1,0:T(8,128)(2,1)}, bf16[528,128]{1,0:T(8,128)(2,1)S(1)}, u32[]{:S(2)}, u32[]{:S(2)}) collective-permute-start(bf16[528,128]{1,0:T(8,128)(2,1)} %pack.1.refs_0_), channel_id=1, source_target_pairs={{0,16},{1,17},{2,18},{3,19},{4,12},{5,13},{6,14},{7,15},{8,24},{9,... | collective-permute-start | bytes 405512 | tf_op jit(solution)/shard_map/ppermute | solution.py:20
  9.4 1.5 %collective-permute-start = (bf16[528,128]{1,0:T(8,128)(2,1)}, bf16[528,128]{1,0:T(8,128)(2,1)S(1)}, u32[]{:S(2)}, u32[]{:S(2)}) collective-permute-start(bf16[528,128]{1,0:T(8,128)(2,1)} %pack.1.refs_0_), channel_id=1, source_target_pairs={{0,8},{1,9},{2,10},{3,11},{4,20},{5,21},{6,22},{7,23},{8,0},{9,1},... | collective-permute-start | bytes 405512 | tf_op jit(solution)/shard_map/ppermute | solution.py:20
  11.1 3.3 %collective-permute-done.7.refs_8_ = bf16[528,128]{1,0:T(8,128)(2,1)S(1)} collective-permute-done((bf16[528,128]{1,0:T(8,128)(2,1)}, bf16[528,128]{1,0:T(8,128)(2,1)S(1)}, u32[]{:S(2)}, u32[]{:S(2)}) %collective-permute-start.7) | collective-permute-done | bytes 135200 | tf_op jit(solution)/shard_map/ppermute | solution.py:20
  14.5 1.5 %collective-permute-start.17 = (bf16[528,128]{1,0:T(8,128)(2,1)S(1)}, bf16[528,128]{1,0:T(8,128)(2,1)S(1)}, u32[]{:S(2)}, u32[]{:S(2)}) collective-permute-start(bf16[528,128]{1,0:T(8,128)(2,1)S(1)} %collective-permute-done.15.refs_16_), channel_id=1, source_target_pairs={{0,16},{1,17},{2,18},{3,19},{4,12},{5,13},{6,14},{7,15},{8,24},{9,... | collective-permute-start | bytes 405512 | tf_op jit(solution)/shard_map/ppermute | solution.py:20
  16.0 1.5 %collective-permute-start.16 = (bf16[528,128]{1,0:T(8,128)(2,1)S(1)}, bf16[528,128]{1,0:T(8,128)(2,1)S(1)}, u32[]{:S(2)}, u32[]{:S(2)}) collective-permute-start(bf16[528,128]{1,0:T(8,128)(2,1)S(1)} %collective-permute-done.15.refs_16_), channel_id=1, source_target_pairs={{0,8},{1,9},{2,10},{3,11},{4,20},{5,21},{6,22},{7,23},{8,0},{9,1},... | collective-permute-start | bytes 405512 | tf_op jit(solution)/shard_map/ppermute | solution.py:20
  17.5 0.4 collective-permute-start.23
  17.9 0.6 %collective-permute-start.9 = (bf16[528,128]{1,0:T(8,128)(2,1)S(1)}, bf16[528,128]{1,0:T(8,128)(2,1)S(1)}, u32[]{:S(2)}, u32[]{:S(2)}) collective-permute-start(bf16[528,128]{1,0:T(8,128)(2,1)S(1)} %collective-permute-done.7.refs_8_), channel_id=1, source_target_pairs={{0,16},{1,17},{2,18},{3,19},{4,12},{5,13},{6,14},{7,15},{8,24},{9,... | collective-permute-start | bytes 405512 | tf_op jit(solution)/shard_map/ppermute | solution.py:20
  18.5 0.9 %collective-permute-done.17.refs_18_ = bf16[528,128]{1,0:T(8,128)(2,1)S(1)} collective-permute-done((bf16[528,128]{1,0:T(8,128)(2,1)S(1)}, bf16[528,128]{1,0:T(8,128)(2,1)S(1)}, u32[]{:S(2)}, u32[]{:S(2)}) %collective-permute-start.17) | collective-permute-done | bytes 135200 | tf_op jit(solution)/shard_map/ppermute | solution.py:20
  19.5 1.5 %collective-permute-start.8 = (bf16[528,128]{1,0:T(8,128)(2,1)S(1)}, bf16[528,128]{1,0:T(8,128)(2,1)S(1)}, u32[]{:S(2)}, u32[]{:S(2)}) collective-permute-start(bf16[528,128]{1,0:T(8,128)(2,1)S(1)} %collective-permute-done.7.refs_8_), channel_id=1, source_target_pairs={{0,8},{1,9},{2,10},{3,11},{4,20},{5,21},{6,22},{7,23},{8,0},{9,1},... | collective-permute-start | bytes 405512 | tf_op jit(solution)/shard_map/ppermute | solution.py:20
  21.0 1.5 %collective-permute-done.23.refs_24_ = bf16[528,128]{1,0:T(8,128)(2,1)S(1)} collective-permute-done((bf16[528,128]{1,0:T(8,128)(2,1)S(1)}, bf16[528,128]{1,0:T(8,128)(2,1)S(1)}, u32[]{:S(2)}, u32[]{:S(2)}) %collective-permute-start.23) | collective-permute-done | bytes 135200 | tf_op jit(solution)/shard_map/ppermute | solution.py:20
  22.5 0.6 %collective-permute-start.2 = (bf16[528,128]{1,0:T(8,128)(2,1)S(1)}, bf16[528,128]{1,0:T(8,128)(2,1)S(1)}, u32[]{:S(2)}, u32[]{:S(2)}) collective-permute-start(bf16[528,128]{1,0:T(8,128)(2,1)S(1)} %collective-permute-done.refs_1_), channel_id=1, source_target_pairs={{0,16},{1,17},{2,18},{3,19},{4,12},{5,13},{6,14},{7,15},{8,24},{9,... | collective-permute-start | bytes 405512 | tf_op jit(solution)/shard_map/ppermute | solution.py:20
  23.1 1.1 %collective-permute-done.9.refs_10_ = bf16[528,128]{1,0:T(8,128)(2,1)S(1)} collective-permute-done((bf16[528,128]{1,0:T(8,128)(2,1)S(1)}, bf16[528,128]{1,0:T(8,128)(2,1)S(1)}, u32[]{:S(2)}, u32[]{:S(2)}) %collective-permute-start.9) | collective-permute-done | bytes 135200 | tf_op jit(solution)/shard_map/ppermute | solution.py:20
  24.2 0.3 collective-permute-done.8.refs_9_
  24.5 0.2 collective-permute-start.20
  24.7 1.4 %collective-permute-start.18 = (bf16[528,128]{1,0:T(8,128)(2,1)S(1)}, bf16[528,128]{1,0:T(8,128)(2,1)S(1)}, u32[]{:S(2)}, u32[]{:S(2)}) collective-permute-start(bf16[528,128]{1,0:T(8,128)(2,1)S(1)} %collective-permute-done.16.refs_17_), channel_id=1, source_target_pairs={{0,16},{1,17},{2,18},{3,19},{4,12},{5,13},{6,14},{7,15},{8,24},{9,... | collective-permute-start | bytes 405512 | tf_op jit(solution)/shard_map/ppermute | solution.py:20
  26.2 1.4 %collective-permute-done.2.refs_3_ = bf16[528,128]{1,0:T(8,128)(2,1)S(1)} collective-permute-done((bf16[528,128]{1,0:T(8,128)(2,1)S(1)}, bf16[528,128]{1,0:T(8,128)(2,1)S(1)}, u32[]{:S(2)}, u32[]{:S(2)}) %collective-permute-start.2) | collective-permute-done | bytes 135200 | tf_op jit(solution)/shard_map/ppermute | solution.py:20
  27.6 0.5 %collective-permute-start.25 = (bf16[528,128]{1,0:T(8,128)(2,1)S(1)}, bf16[528,128]{1,0:T(8,128)(2,1)S(1)}, u32[]{:S(2)}, u32[]{:S(2)}) collective-permute-start(bf16[528,128]{1,0:T(8,128)(2,1)S(1)} %collective-permute-done.23.refs_24_), channel_id=1, source_target_pairs={{0,16},{1,17},{2,18},{3,19},{4,12},{5,13},{6,14},{7,15},{8,24},{9,... | collective-permute-start | bytes 405512 | tf_op jit(solution)/shard_map/ppermute | solution.py:20
  28.1 1.4 %collective-permute-start.24 = (bf16[528,128]{1,0:T(8,128)(2,1)S(1)}, bf16[528,128]{1,0:T(8,128)(2,1)S(1)}, u32[]{:S(2)}, u32[]{:S(2)}) collective-permute-start(bf16[528,128]{1,0:T(8,128)(2,1)S(1)} %collective-permute-done.23.refs_24_), channel_id=1, source_target_pairs={{0,8},{1,9},{2,10},{3,11},{4,20},{5,21},{6,22},{7,23},{8,0},{9,1},... | collective-permute-start | bytes 405512 | tf_op jit(solution)/shard_map/ppermute | solution.py:20
  29.5 0.2 collective-permute-done.18.refs_19_
  29.7 0.3 collective-permute-start.12
  30.1 1.5 %collective-permute-start.10 = (bf16[528,128]{1,0:T(8,128)(2,1)S(1)}, bf16[528,128]{1,0:T(8,128)(2,1)S(1)}, u32[]{:S(2)}, u32[]{:S(2)}) collective-permute-start(bf16[528,128]{1,0:T(8,128)(2,1)S(1)} %collective-permute-done.8.refs_9_), channel_id=1, source_target_pairs={{0,16},{1,17},{2,18},{3,19},{4,12},{5,13},{6,14},{7,15},{8,24},{9,... | collective-permute-start | bytes 405512 | tf_op jit(solution)/shard_map/ppermute | solution.py:20
  31.6 2.0 %collective-permute-done.25.refs_26_ = bf16[528,128]{1,0:T(8,128)(2,1)S(1)} collective-permute-done((bf16[528,128]{1,0:T(8,128)(2,1)S(1)}, bf16[528,128]{1,0:T(8,128)(2,1)S(1)}, u32[]{:S(2)}, u32[]{:S(2)}) %collective-permute-start.25) | collective-permute-done | bytes 135200 | tf_op jit(solution)/shard_map/ppermute | solution.py:20
  33.6 1.0 %collective-permute-start.26 = (bf16[528,128]{1,0:T(8,128)(2,1)S(1)}, bf16[528,128]{1,0:T(8,128)(2,1)S(1)}, u32[]{:S(2)}, u32[]{:S(2)}) collective-permute-start(bf16[528,128]{1,0:T(8,128)(2,1)S(1)} %collective-permute-done.24.refs_25_), channel_id=1, source_target_pairs={{0,16},{1,17},{2,18},{3,19},{4,12},{5,13},{6,14},{7,15},{8,24},{9,... | collective-permute-start | bytes 405512 | tf_op jit(solution)/shard_map/ppermute | solution.py:20
  34.7 0.5 %collective-permute-start.22 = (bf16[528,128]{1,0:T(8,128)(2,1)S(1)}, bf16[528,128]{1,0:T(8,128)(2,1)S(1)}, u32[]{:S(2)}, u32[]{:S(2)}) collective-permute-start(bf16[528,128]{1,0:T(8,128)(2,1)S(1)} %collective-permute-done.18.refs_19_), channel_id=1, source_target_pairs={{0,4},{1,5},{2,6},{3,7},{4,0},{5,1},{6,2},{7,3},{8,12},{9,13},{10,... | collective-permute-start | bytes 405512 | tf_op jit(solution)/shard_map/ppermute | solution.py:20
  35.3 0.4 collective-permute-start.14
  35.7 3.0 %collective-permute-done.26.refs_27_ = bf16[528,128]{1,0:T(8,128)(2,1)S(1)} collective-permute-done((bf16[528,128]{1,0:T(8,128)(2,1)S(1)}, bf16[528,128]{1,0:T(8,128)(2,1)S(1)}, u32[]{:S(2)}, u32[]{:S(2)}) %collective-permute-start.26) | collective-permute-done | bytes 135200 | tf_op jit(solution)/shard_map/ppermute | solution.py:20
  38.8 1.3 %collective-permute-done.30.refs_31_ = bf16[528,128]{1,0:T(8,128)(2,1)S(1)} collective-permute-done((bf16[528,128]{1,0:T(8,128)(2,1)S(1)}, bf16[528,128]{1,0:T(8,128)(2,1)S(1)}, u32[]{:S(2)}, u32[]{:S(2)}) %collective-permute-start.30) | collective-permute-done | bytes 135200 | tf_op jit(solution)/shard_map/ppermute | solution.py:20
  40.3 0.7 %copy-done.30 = bf16[528,128]{1,0:T(8,128)(2,1)} copy-done((bf16[528,128]{1,0:T(8,128)(2,1)}, bf16[528,128]{1,0:T(8,128)(2,1)S(1)}, u32[]{:S(2)}) %copy-start.30) | copy-done | bytes 135192
  41.0 6.3 %finish.1 = (f32[128,1024]{1,0:T(8,128)}, f32[128]{0:T(128)}) custom-call(bf16[128,1024]{1,0:T(8,128)(2,1)} %queries_ref.1, s32[1,256]{1,0:T(1,128)} %pattern_ref.1, s32[128]{0:T(128)} %positives_ref.1, f32[128]{0:T(128)} %multiplier_ref.1, bf16[528,128]{1,0:T(8,128)(2,1)} %pack.1.refs_0_, bf16[528,128]{1,0:T(8,128)(2,1)} %copy-done.4, ...), custom_call_target="tpu_custom_call" | custom-call | tf_op jit(solution)/shard_map/finish/pallas_call | solution.py:133
  (94 shorter events, 0.6 us)
Async XLA Ops:
  2.3 8.8 %collective-permute-start.15 = (bf16[528,128]{1,0:T(8,128)(2,1)}, bf16[528,128]{1,0:T(8,128)(2,1)S(1)}, u32[]{:S(2)}, u32[]{:S(2)}) collective-permute-start(bf16[528,128]{1,0:T(8,128)(2,1)} %pack.1.refs_0_), channel_id=1, source_target_pairs={{0,1},{1,0},{2,3},{3,2},{4,5},{5,4},{6,7},{7,6},{8,9},{9,8},{10,11... | collective-permute-start | bytes 405512 | tf_op jit(solution)/shard_map/ppermute | solution.py:20
  5.3 9.1 %collective-permute-start.7 = (bf16[528,128]{1,0:T(8,128)(2,1)}, bf16[528,128]{1,0:T(8,128)(2,1)S(1)}, u32[]{:S(2)}, u32[]{:S(2)}) collective-permute-start(bf16[528,128]{1,0:T(8,128)(2,1)} %pack.1.refs_0_), channel_id=1, source_target_pairs={{0,2},{1,3},{2,0},{3,1},{4,6},{5,7},{6,4},{7,5},{8,10},{9,11},{10,... | collective-permute-start | bytes 405512 | tf_op jit(solution)/shard_map/ppermute | solution.py:20
  7.9 8.1 %collective-permute-start.3 = (bf16[528,128]{1,0:T(8,128)(2,1)}, bf16[528,128]{1,0:T(8,128)(2,1)S(1)}, u32[]{:S(2)}, u32[]{:S(2)}) collective-permute-start(bf16[528,128]{1,0:T(8,128)(2,1)} %pack.1.refs_0_), channel_id=1, source_target_pairs={{0,4},{1,5},{2,6},{3,7},{4,0},{5,1},{6,2},{7,3},{8,12},{9,13},{10,... | collective-permute-start | bytes 405512 | tf_op jit(solution)/shard_map/ppermute | solution.py:20
  7.9 9.5 %collective-permute-start.1 = (bf16[528,128]{1,0:T(8,128)(2,1)}, bf16[528,128]{1,0:T(8,128)(2,1)S(1)}, u32[]{:S(2)}, u32[]{:S(2)}) collective-permute-start(bf16[528,128]{1,0:T(8,128)(2,1)} %pack.1.refs_0_), channel_id=1, source_target_pairs={{0,16},{1,17},{2,18},{3,19},{4,12},{5,13},{6,14},{7,15},{8,24},{9,... | collective-permute-start | bytes 405512 | tf_op jit(solution)/shard_map/ppermute | solution.py:20
  9.4 8.5 %collective-permute-start = (bf16[528,128]{1,0:T(8,128)(2,1)}, bf16[528,128]{1,0:T(8,128)(2,1)S(1)}, u32[]{:S(2)}, u32[]{:S(2)}) collective-permute-start(bf16[528,128]{1,0:T(8,128)(2,1)} %pack.1.refs_0_), channel_id=1, source_target_pairs={{0,8},{1,9},{2,10},{3,11},{4,20},{5,21},{6,22},{7,23},{8,0},{9,1},... | collective-permute-start | bytes 405512 | tf_op jit(solution)/shard_map/ppermute | solution.py:20
  11.1 28.9 %copy-start = (bf16[528,128]{1,0:T(8,128)(2,1)}, bf16[528,128]{1,0:T(8,128)(2,1)S(1)}, u32[]{:S(2)}) copy-start(bf16[528,128]{1,0:T(8,128)(2,1)S(1)} %collective-permute-done.15.refs_16_) | copy-start | bytes 405508
  11.1 6.8 %collective-permute-start.19 = (bf16[528,128]{1,0:T(8,128)(2,1)S(1)}, bf16[528,128]{1,0:T(8,128)(2,1)S(1)}, u32[]{:S(2)}, u32[]{:S(2)}) collective-permute-start(bf16[528,128]{1,0:T(8,128)(2,1)S(1)} %collective-permute-done.15.refs_16_), channel_id=1, source_target_pairs={{0,4},{1,5},{2,6},{3,7},{4,0},{5,1},{6,2},{7,3},{8,12},{9,13},{10,... | collective-permute-start | bytes 405512 | tf_op jit(solution)/shard_map/ppermute | solution.py:20
  14.5 5.0 %collective-permute-start.17 = (bf16[528,128]{1,0:T(8,128)(2,1)S(1)}, bf16[528,128]{1,0:T(8,128)(2,1)S(1)}, u32[]{:S(2)}, u32[]{:S(2)}) collective-permute-start(bf16[528,128]{1,0:T(8,128)(2,1)S(1)} %collective-permute-done.15.refs_16_), channel_id=1, source_target_pairs={{0,16},{1,17},{2,18},{3,19},{4,12},{5,13},{6,14},{7,15},{8,24},{9,... | collective-permute-start | bytes 405512 | tf_op jit(solution)/shard_map/ppermute | solution.py:20
  16.0 5.0 %collective-permute-start.16 = (bf16[528,128]{1,0:T(8,128)(2,1)S(1)}, bf16[528,128]{1,0:T(8,128)(2,1)S(1)}, u32[]{:S(2)}, u32[]{:S(2)}) collective-permute-start(bf16[528,128]{1,0:T(8,128)(2,1)S(1)} %collective-permute-done.15.refs_16_), channel_id=1, source_target_pairs={{0,8},{1,9},{2,10},{3,11},{4,20},{5,21},{6,22},{7,23},{8,0},{9,1},... | collective-permute-start | bytes 405512 | tf_op jit(solution)/shard_map/ppermute | solution.py:20
  17.5 5.0 %collective-permute-start.23 = (bf16[528,128]{1,0:T(8,128)(2,1)S(1)}, bf16[528,128]{1,0:T(8,128)(2,1)S(1)}, u32[]{:S(2)}, u32[]{:S(2)}) collective-permute-start(bf16[528,128]{1,0:T(8,128)(2,1)S(1)} %collective-permute-done.7.refs_8_), channel_id=1, source_target_pairs={{0,1},{1,0},{2,3},{3,2},{4,5},{5,4},{6,7},{7,6},{8,9},{9,8},{10,11... | collective-permute-start | bytes 405512 | tf_op jit(solution)/shard_map/ppermute | solution.py:20
  17.9 4.6 %collective-permute-start.11 = (bf16[528,128]{1,0:T(8,128)(2,1)S(1)}, bf16[528,128]{1,0:T(8,128)(2,1)S(1)}, u32[]{:S(2)}, u32[]{:S(2)}) collective-permute-start(bf16[528,128]{1,0:T(8,128)(2,1)S(1)} %collective-permute-done.7.refs_8_), channel_id=1, source_target_pairs={{0,4},{1,5},{2,6},{3,7},{4,0},{5,1},{6,2},{7,3},{8,12},{9,13},{10,... | collective-permute-start | bytes 405512 | tf_op jit(solution)/shard_map/ppermute | solution.py:20
  17.9 6.2 %collective-permute-start.9 = (bf16[528,128]{1,0:T(8,128)(2,1)S(1)}, bf16[528,128]{1,0:T(8,128)(2,1)S(1)}, u32[]{:S(2)}, u32[]{:S(2)}) collective-permute-start(bf16[528,128]{1,0:T(8,128)(2,1)S(1)} %collective-permute-done.7.refs_8_), channel_id=1, source_target_pairs={{0,16},{1,17},{2,18},{3,19},{4,12},{5,13},{6,14},{7,15},{8,24},{9,... | collective-permute-start | bytes 405512 | tf_op jit(solution)/shard_map/ppermute | solution.py:20
  19.5 5.0 %collective-permute-start.8 = (bf16[528,128]{1,0:T(8,128)(2,1)S(1)}, bf16[528,128]{1,0:T(8,128)(2,1)S(1)}, u32[]{:S(2)}, u32[]{:S(2)}) collective-permute-start(bf16[528,128]{1,0:T(8,128)(2,1)S(1)} %collective-permute-done.7.refs_8_), channel_id=1, source_target_pairs={{0,8},{1,9},{2,10},{3,11},{4,20},{5,21},{6,22},{7,23},{8,0},{9,1},... | collective-permute-start | bytes 405512 | tf_op jit(solution)/shard_map/ppermute | solution.py:20
  21.0 3.7 %collective-permute-start.5 = (bf16[528,128]{1,0:T(8,128)(2,1)S(1)}, bf16[528,128]{1,0:T(8,128)(2,1)S(1)}, u32[]{:S(2)}, u32[]{:S(2)}) collective-permute-start(bf16[528,128]{1,0:T(8,128)(2,1)S(1)} %collective-permute-done.1.refs_2_), channel_id=1, source_target_pairs={{0,4},{1,5},{2,6},{3,7},{4,0},{5,1},{6,2},{7,3},{8,12},{9,13},{10,... | collective-permute-start | bytes 405512 | tf_op jit(solution)/shard_map/ppermute | solution.py:20
  22.5 3.6 %collective-permute-start.4 = (bf16[528,128]{1,0:T(8,128)(2,1)S(1)}, bf16[528,128]{1,0:T(8,128)(2,1)S(1)}, u32[]{:S(2)}, u32[]{:S(2)}) collective-permute-start(bf16[528,128]{1,0:T(8,128)(2,1)S(1)} %collective-permute-done.refs_1_), channel_id=1, source_target_pairs={{0,4},{1,5},{2,6},{3,7},{4,0},{5,1},{6,2},{7,3},{8,12},{9,13},{10,... | collective-permute-start | bytes 405512 | tf_op jit(solution)/shard_map/ppermute | solution.py:20
  22.5 5.1 %collective-permute-start.2 = (bf16[528,128]{1,0:T(8,128)(2,1)S(1)}, bf16[528,128]{1,0:T(8,128)(2,1)S(1)}, u32[]{:S(2)}, u32[]{:S(2)}) collective-permute-start(bf16[528,128]{1,0:T(8,128)(2,1)S(1)} %collective-permute-done.refs_1_), channel_id=1, source_target_pairs={{0,16},{1,17},{2,18},{3,19},{4,12},{5,13},{6,14},{7,15},{8,24},{9,... | collective-permute-start | bytes 405512 | tf_op jit(solution)/shard_map/ppermute | solution.py:20
  24.2 3.9 %collective-permute-start.21 = (bf16[528,128]{1,0:T(8,128)(2,1)S(1)}, bf16[528,128]{1,0:T(8,128)(2,1)S(1)}, u32[]{:S(2)}, u32[]{:S(2)}) collective-permute-start(bf16[528,128]{1,0:T(8,128)(2,1)S(1)} %collective-permute-done.17.refs_18_), channel_id=1, source_target_pairs={{0,4},{1,5},{2,6},{3,7},{4,0},{5,1},{6,2},{7,3},{8,12},{9,13},{10,... | collective-permute-start | bytes 405512 | tf_op jit(solution)/shard_map/ppermute | solution.py:20
  24.5 5.1 %collective-permute-start.20 = (bf16[528,128]{1,0:T(8,128)(2,1)S(1)}, bf16[528,128]{1,0:T(8,128)(2,1)S(1)}, u32[]{:S(2)}, u32[]{:S(2)}) collective-permute-start(bf16[528,128]{1,0:T(8,128)(2,1)S(1)} %collective-permute-done.16.refs_17_), channel_id=1, source_target_pairs={{0,4},{1,5},{2,6},{3,7},{4,0},{5,1},{6,2},{7,3},{8,12},{9,13},{10,... | collective-permute-start | bytes 405512 | tf_op jit(solution)/shard_map/ppermute | solution.py:20
  24.7 5.0 %collective-permute-start.18 = (bf16[528,128]{1,0:T(8,128)(2,1)S(1)}, bf16[528,128]{1,0:T(8,128)(2,1)S(1)}, u32[]{:S(2)}, u32[]{:S(2)}) collective-permute-start(bf16[528,128]{1,0:T(8,128)(2,1)S(1)} %collective-permute-done.16.refs_17_), channel_id=1, source_target_pairs={{0,16},{1,17},{2,18},{3,19},{4,12},{5,13},{6,14},{7,15},{8,24},{9,... | collective-permute-start | bytes 405512 | tf_op jit(solution)/shard_map/ppermute | solution.py:20
  26.1 4.0 %collective-permute-start.27 = (bf16[528,128]{1,0:T(8,128)(2,1)S(1)}, bf16[528,128]{1,0:T(8,128)(2,1)S(1)}, u32[]{:S(2)}, u32[]{:S(2)}) collective-permute-start(bf16[528,128]{1,0:T(8,128)(2,1)S(1)} %collective-permute-done.23.refs_24_), channel_id=1, source_target_pairs={{0,4},{1,5},{2,6},{3,7},{4,0},{5,1},{6,2},{7,3},{8,12},{9,13},{10,... | collective-permute-start | bytes 405512 | tf_op jit(solution)/shard_map/ppermute | solution.py:20
  27.6 6.0 %collective-permute-start.25 = (bf16[528,128]{1,0:T(8,128)(2,1)S(1)}, bf16[528,128]{1,0:T(8,128)(2,1)S(1)}, u32[]{:S(2)}, u32[]{:S(2)}) collective-permute-start(bf16[528,128]{1,0:T(8,128)(2,1)S(1)} %collective-permute-done.23.refs_24_), channel_id=1, source_target_pairs={{0,16},{1,17},{2,18},{3,19},{4,12},{5,13},{6,14},{7,15},{8,24},{9,... | collective-permute-start | bytes 405512 | tf_op jit(solution)/shard_map/ppermute | solution.py:20
  28.1 5.5 %collective-permute-start.24 = (bf16[528,128]{1,0:T(8,128)(2,1)S(1)}, bf16[528,128]{1,0:T(8,128)(2,1)S(1)}, u32[]{:S(2)}, u32[]{:S(2)}) collective-permute-start(bf16[528,128]{1,0:T(8,128)(2,1)S(1)} %collective-permute-done.23.refs_24_), channel_id=1, source_target_pairs={{0,8},{1,9},{2,10},{3,11},{4,20},{5,21},{6,22},{7,23},{8,0},{9,1},... | collective-permute-start | bytes 405512 | tf_op jit(solution)/shard_map/ppermute | solution.py:20
  29.5 5.1 %collective-permute-start.13 = (bf16[528,128]{1,0:T(8,128)(2,1)S(1)}, bf16[528,128]{1,0:T(8,128)(2,1)S(1)}, u32[]{:S(2)}, u32[]{:S(2)}) collective-permute-start(bf16[528,128]{1,0:T(8,128)(2,1)S(1)} %collective-permute-done.9.refs_10_), channel_id=1, source_target_pairs={{0,4},{1,5},{2,6},{3,7},{4,0},{5,1},{6,2},{7,3},{8,12},{9,13},{10,... | collective-permute-start | bytes 405512 | tf_op jit(solution)/shard_map/ppermute | solution.py:20
  29.7 4.9 %collective-permute-start.12 = (bf16[528,128]{1,0:T(8,128)(2,1)S(1)}, bf16[528,128]{1,0:T(8,128)(2,1)S(1)}, u32[]{:S(2)}, u32[]{:S(2)}) collective-permute-start(bf16[528,128]{1,0:T(8,128)(2,1)S(1)} %collective-permute-done.8.refs_9_), channel_id=1, source_target_pairs={{0,4},{1,5},{2,6},{3,7},{4,0},{5,1},{6,2},{7,3},{8,12},{9,13},{10,... | collective-permute-start | bytes 405512 | tf_op jit(solution)/shard_map/ppermute | solution.py:20
  30.1 5.1 %collective-permute-start.10 = (bf16[528,128]{1,0:T(8,128)(2,1)S(1)}, bf16[528,128]{1,0:T(8,128)(2,1)S(1)}, u32[]{:S(2)}, u32[]{:S(2)}) collective-permute-start(bf16[528,128]{1,0:T(8,128)(2,1)S(1)} %collective-permute-done.8.refs_9_), channel_id=1, source_target_pairs={{0,16},{1,17},{2,18},{3,19},{4,12},{5,13},{6,14},{7,15},{8,24},{9,... | collective-permute-start | bytes 405512 | tf_op jit(solution)/shard_map/ppermute | solution.py:20
  33.6 1.6 %collective-permute-start.6 = (bf16[528,128]{1,0:T(8,128)(2,1)S(1)}, bf16[528,128]{1,0:T(8,128)(2,1)S(1)}, u32[]{:S(2)}, u32[]{:S(2)}) collective-permute-start(bf16[528,128]{1,0:T(8,128)(2,1)S(1)} %collective-permute-done.2.refs_3_), channel_id=1, source_target_pairs={{0,4},{1,5},{2,6},{3,7},{4,0},{5,1},{6,2},{7,3},{8,12},{9,13},{10,... | collective-permute-start | bytes 405512 | tf_op jit(solution)/shard_map/ppermute | solution.py:20
  33.6 5.1 %collective-permute-start.26 = (bf16[528,128]{1,0:T(8,128)(2,1)S(1)}, bf16[528,128]{1,0:T(8,128)(2,1)S(1)}, u32[]{:S(2)}, u32[]{:S(2)}) collective-permute-start(bf16[528,128]{1,0:T(8,128)(2,1)S(1)} %collective-permute-done.24.refs_25_), channel_id=1, source_target_pairs={{0,16},{1,17},{2,18},{3,19},{4,12},{5,13},{6,14},{7,15},{8,24},{9,... | collective-permute-start | bytes 405512 | tf_op jit(solution)/shard_map/ppermute | solution.py:20
  34.6 4.1 %collective-permute-start.28 = (bf16[528,128]{1,0:T(8,128)(2,1)S(1)}, bf16[528,128]{1,0:T(8,128)(2,1)S(1)}, u32[]{:S(2)}, u32[]{:S(2)}) collective-permute-start(bf16[528,128]{1,0:T(8,128)(2,1)S(1)} %collective-permute-done.24.refs_25_), channel_id=1, source_target_pairs={{0,4},{1,5},{2,6},{3,7},{4,0},{5,1},{6,2},{7,3},{8,12},{9,13},{10,... | collective-permute-start | bytes 405512 | tf_op jit(solution)/shard_map/ppermute | solution.py:20
  34.7 4.0 %collective-permute-start.22 = (bf16[528,128]{1,0:T(8,128)(2,1)S(1)}, bf16[528,128]{1,0:T(8,128)(2,1)S(1)}, u32[]{:S(2)}, u32[]{:S(2)}) collective-permute-start(bf16[528,128]{1,0:T(8,128)(2,1)S(1)} %collective-permute-done.18.refs_19_), channel_id=1, source_target_pairs={{0,4},{1,5},{2,6},{3,7},{4,0},{5,1},{6,2},{7,3},{8,12},{9,13},{10,... | collective-permute-start | bytes 405512 | tf_op jit(solution)/shard_map/ppermute | solution.py:20
  35.2 3.6 %collective-permute-start.29 = (bf16[528,128]{1,0:T(8,128)(2,1)S(1)}, bf16[528,128]{1,0:T(8,128)(2,1)S(1)}, u32[]{:S(2)}, u32[]{:S(2)}) collective-permute-start(bf16[528,128]{1,0:T(8,128)(2,1)S(1)} %collective-permute-done.25.refs_26_), channel_id=1, source_target_pairs={{0,4},{1,5},{2,6},{3,7},{4,0},{5,1},{6,2},{7,3},{8,12},{9,13},{10,... | collective-permute-start | bytes 405512 | tf_op jit(solution)/shard_map/ppermute | solution.py:20
  35.3 3.5 %collective-permute-start.14 = (bf16[528,128]{1,0:T(8,128)(2,1)S(1)}, bf16[528,128]{1,0:T(8,128)(2,1)S(1)}, u32[]{:S(2)}, u32[]{:S(2)}) collective-permute-start(bf16[528,128]{1,0:T(8,128)(2,1)S(1)} %collective-permute-done.10.refs_11_), channel_id=1, source_target_pairs={{0,4},{1,5},{2,6},{3,7},{4,0},{5,1},{6,2},{7,3},{8,12},{9,13},{10,... | collective-permute-start | bytes 405512 | tf_op jit(solution)/shard_map/ppermute | solution.py:20
  38.7 1.4 %collective-permute-start.30 = (bf16[528,128]{1,0:T(8,128)(2,1)S(1)}, bf16[528,128]{1,0:T(8,128)(2,1)S(1)}, u32[]{:S(2)}, u32[]{:S(2)}) collective-permute-start(bf16[528,128]{1,0:T(8,128)(2,1)S(1)} %collective-permute-done.26.refs_27_), channel_id=1, source_target_pairs={{0,4},{1,5},{2,6},{3,7},{4,0},{5,1},{6,2},{7,3},{8,12},{9,13},{10,... | collective-permute-start | bytes 405512 | tf_op jit(solution)/shard_map/ppermute | solution.py:20
  (30 other events, 351.9 us)

commit v2 on v1

--- a/solution.py
+++ b/solution.py
@@ -42,15 +42,19 @@
     rows, width = keys.shape
     return pl.pallas_call(
         pack_kernel,
-        out_shape=jax.ShapeDtypeStruct((width // LANES * rows + TAG_ROWS, LANES), jnp.bfloat16),
+        out_shape=pltpu.VMEM((width // LANES * rows + TAG_ROWS, LANES), jnp.bfloat16),
         in_specs=[VMEM, VMEM],
         out_specs=VMEM,
         name="pack",
     )(keys, clusters)
 
 
-def main_kernel(rows, group, queries_ref, pattern_ref, positives_ref, multiplier_ref, *refs):
-    wires, (grad_ref, loss_ref, key_ref) = refs[:-3], refs[-3:]
+def sum_kernel(rows, group, closing, priors, queries_ref, pattern_ref, positives_ref, *refs):
+    refs = list(refs)
+    multiplier_ref = refs.pop(0) if closing else None
+    prior_refs = [(refs.pop(0), refs.pop(0)) for _ in range(priors)]
+    key_ref, out_b, out_a = refs.pop(), refs.pop(), refs.pop()
+    wires = refs
     count, width = queries_ref.shape
     tiles = width // LANES
     per = LANES // rows
@@ -68,7 +72,6 @@
     scale = lax.rsqrt(jnp.sum(floats * floats, axis=1, keepdims=True) + epsilon)
     unit = (floats * scale).astype(jnp.bfloat16)
     positive = as_column(positives_ref[...].reshape(1, count).astype(jnp.float32))
-    multiplier = as_column(multiplier_ref[...].reshape(1, count))
     clusters_all = pattern_ref.shape[1]
     marks = jnp.broadcast_to(
         pattern_ref[...].astype(jnp.float32).astype(jnp.bfloat16), (16, clusters_all)
@@ -117,62 +120,107 @@
         )
 
     parts = [absorb(shards[first : first + group]) for first in range(0, len(shards), group)]
+    for stats_ref, sums_ref in prior_refs:
+        parts.append((stats_ref[:, 0:1], stats_ref[:, 1:2], sums_ref[...]))
     totals, positive_score, sums = (functools.reduce(jnp.add, column) for column in zip(*parts))
+    if not closing:
+        out_a[...] = jnp.where(lane == 0, totals, jnp.where(lane == 1, positive_score, 0.0))
+        out_b[...] = sums
+        return
+    multiplier = as_column(multiplier_ref[...].reshape(1, count))
     direction = sums[:count] / totals - sums[count:]
     gradient = direction * (multiplier / logit_divisor)
     projection = jnp.sum(floats * gradient, axis=1, keepdims=True)
-    grad_ref[...] = scale * gradient - scale * scale * scale * floats * projection
+    out_a[...] = scale * gradient - scale * scale * scale * floats * projection
     loss = jnp.log(totals) - positive_score
-    loss_ref[...] = jnp.sum(jnp.where(diagonal, loss, 0.0), axis=0, keepdims=True).reshape(count)
-
-
-def finish(rows, queries, pattern, positives, multiplier, wires):
+    out_b[...] = jnp.sum(jnp.where(diagonal, loss, 0.0), axis=0, keepdims=True).reshape(count)
+
+
+def sum_spans(rows, queries, pattern, positives, wires, multiplier=None, priors=(), cost=None):
     count, width = queries.shape
     wire_rows = width // LANES * rows + TAG_ROWS
     group = min(32, sum(wire.shape[0] // wire_rows for wire in wires))
+    closing = multiplier is not None
+    if closing:
+        shapes = ((count, width), (count,))
+    else:
+        shapes = ((count, LANES), (2 * count, width))
+    operands = [queries, pattern, positives] + [multiplier] * closing
+    operands += [part for prior in priors for part in prior] + list(wires)
     return pl.pallas_call(
-        functools.partial(main_kernel, rows, group),
-        out_shape=(
-            jax.ShapeDtypeStruct((count, width), jnp.float32),
-            jax.ShapeDtypeStruct((count,), jnp.float32),
-        ),
-        in_specs=[VMEM] * (4 + len(wires)),
+        functools.partial(sum_kernel, rows, group, closing, len(priors)),
+        out_shape=tuple(jax.ShapeDtypeStruct(shape, jnp.float32) for shape in shapes),
+        in_specs=[VMEM] * len(operands),
         out_specs=(VMEM, VMEM),
         scratch_shapes=[pltpu.VMEM((group * rows, width), jnp.bfloat16)],
-        compiler_params=pltpu.CompilerParams(vmem_limit_bytes=56 * 1024 * 1024),
-        name="finish",
-    )(queries, pattern, positives, multiplier, *wires)
+        compiler_params=pltpu.CompilerParams(vmem_limit_bytes=24 * 1024 * 1024),
+        cost_estimate=cost and pl.CostEstimate(flops=cost, bytes_accessed=0, transcendentals=0),
+        name="close" if closing else "sum_spans",
+    )(*operands)
 
 
 def body(counts, queries, keys, pattern, clusters, positives, loss_multiplier):
     dp, index = counts
     rows = keys.shape[0]
-    index_bits = index.bit_length() - 1
-    dp_bits = dp.bit_length() - 1
-    core = index_bits
-    plane = list(range(index_bits + 1, index_bits + dp_bits))
+    core = index.bit_length() - 1
+    plane = list(range(core + 1, core + dp.bit_length() - 1))
+    far = list(range(1, core))
 
     def along(value, bit):
         return exchange(value, counts, lambda i: i ^ (1 << bit))
 
-    def along_plane(value, step):
-        first, second = plane[step], plane[len(plane) - 1 - step]
-        return exchange(
-            value, counts, lambda i: i ^ (1 << (second if (i >> core) & 1 else first))
-        )
-
-    column = [pack(keys, clusters)]
-    for bit in reversed(range(index_bits)):
-        column += [along(value, bit) for value in column]
-    if len(column) > 4:
-        column = [jnp.concatenate(column, axis=0)]
-    held = []
-    for value in column:
-        block = [value]
-        for step in range(len(plane)):
-            block += [along_plane(item, step) for item in block]
-        held += block + [along(item, core) for item in block]
-    return finish(rows, queries, pattern, positives, loss_multiplier, held)
+    def join(values):
+        return values[0] if len(values) == 1 else jnp.concatenate(values, axis=0)
+
+    def both(values):
+        value = join(values)
+        return [value, along(value, core)]
+
+    own = pack(keys, clusters)
+    unit = own.shape[0]
+    args = (rows, queries, pattern, positives)
+    if len(plane) != 2 or len(far) != 1:
+        return doubling(counts, args, own, loss_multiplier)
+
+    bits = {1: plane[0], 2: plane[1], 4: 0, 8: far[0]}
+
+    def go(value, *ways):
+        flips = [sum(1 << place for bit, place in bits.items() if way & bit) for way in ways]
+        return exchange(value, counts, lambda i: i ^ flips[(i >> core) & 1])
+
+    def after(value, *earlier):
+        return lax.optimization_barrier((value, *earlier))[0]
+
+    v0 = own
+    v1 = go(v0, 1, 2)
+    v2_3 = go(join([v0, v1]), 2, 1)
+    v4 = go(v0, 4, 4)
+    v5 = go(v4, 1, 2)
+    v6_7 = go(join([v4, v5]), 2, 1)
+    v8 = go(v0, 8, 8)
+    v9 = go(after(v8, v4), 1, 2)
+    v10 = go(v8, 2, 1)
+    v12 = go(v8, 4, 4)
+    v14_11 = go(after(join([v12, v9]), v2_3), 2, 1)
+    v13 = go(v9, 4, 4)
+    v15 = go(after(v10, v10), 5, 6)
+    part = sum_spans(*args, both([v0, v2_3, v4, v8, v9, v10]), cost=int(10000000000.0))
+    return sum_spans(*args, both([v6_7, v14_11]) + both([v1, v5, v12, v13]) + both([v15]), loss_multiplier, [part])
+
+
+def doubling(counts, args, own, loss_multiplier):
+    dp, index = counts
+    held = [own]
+    for bit in range((dp * index).bit_length() - 1):
+        if bit < index.bit_length() - 1:
+            value = jnp.concatenate(held, axis=0) if len(held) > 1 else held[0]
+            held = [value, exchange(value, counts, lambda i: i ^ (1 << bit))]
+        else:
+            if len(held) == 2 and bit == index.bit_length() - 1:
+                held = [jnp.concatenate(held, axis=0)]
+            held = held + [exchange(value, counts, lambda i: i ^ (1 << bit)) for value in held]
+    parts = [sum_spans(*args, held[n : n + 4]) for n in range(4, len(held), 4)]
+    return sum_spans(*args, held[:4], loss_multiplier, parts)
 
 
 def solution(mesh):

time: 47.5 us -> 35.9 us (0.76)
  waiting for transfers between devices: 15.3 us -> 9.4 us
  starting transfers between devices: 22.3 us -> 19.2 us
  Pallas kernels: 8.01 us -> 5.41 us
    ppermute x31 -> x16, waiting for transfers between devices: 15.3 us -> 9.4 us  [exchange(): return lax.ppermute(value, AXES, [(i, flip(i)) for i in range(total)])]
    ppermute x31 -> x16, starting transfers between devices: 22.3 us -> 19.2 us  [exchange(): return lax.ppermute(value, AXES, [(i, flip(i)) for i in range(total)])]
    pallas_call x2 -> x3, Pallas kernels: 8.01 us -> 5.41 us  [the longest x2 4.38 us: sum_spans(): pl.pallas_call(functools.partial(sum_kernel, rows, group, closing, len(pr...]
  transfers between devices with their start and end apart: 31 -> 16, of which waited for: 11 -> 6; matrix products, arithmetic and copies ran while one was open for 0% -> 1% of each run, Pallas kernels for 0% -> 4%
where the time goes in v2:
time: 35.9 us; the launch traced here: 35.8 us
  starting transfers between devices  19.2 us (53%)
  waiting for transfers between devices  9.4 us (26%)
  Pallas kernels  5.41 us (15%)
  local copies, waits for them, and re-layouts  0.92 us (3%)
  between operations  0.84 us (2%)
    ppermute x16, starting transfers between devices, exchange(): return lax.ppermute(value, AXES, [(i, flip(i)) for i in range(total)])  19.2 us
    ppermute x16, waiting for transfers between devices, exchange(): return lax.ppermute(value, AXES, [(i, flip(i)) for i in range(total)])  9.4 us
    pallas_call x2, Pallas kernels, sum_spans(): pl.pallas_call(functools.partial(sum_kernel, rows, group, closing, len(pr...  4.38 us
    pallas_call x1, Pallas kernels, pack(): pl.pallas_call(pack_kernel, out_shape=pltpu.VMEM((width // LANES * rows +...  1.02 us
    unnamed x17, local copies, waits for them, and re-layouts  0.85 us
  transfers between devices with their start and end apart: 16, of which 6 were waited for; matrix products, arithmetic and copies ran while one was open for 1% of the time, Pallas kernels for 4%

profile of v2, /device:TPU:0, one launch (start us, length us, event | category | flops | bytes accessed | tf_op | source)
XLA Modules:
  0.0 35.8 jit_solution(6109304066107425005)
XLA Ops:
  0.6 1.0 %pack.1 = bf16[528,128]{1,0:T(8,128)(2,1)S(1)} custom-call(bf16[64,1024]{1,0:T(8,128)(2,1)} %keys_ref.1, s32[64]{0:T(128)} %clusters_ref.1), custom_call_target="tpu_custom_call" | custom-call | tf_op jit(solution)/shard_map/pack/pallas_call | solution.py:43
  1.7 3.1 %collective-permute-start.2 = (bf16[528,128]{1,0:T(8,128)(2,1)S(1)}, bf16[528,128]{1,0:T(8,128)(2,1)S(1)}, u32[]{:S(2)}, u32[]{:S(2)}) collective-permute-start(bf16[528,128]{1,0:T(8,128)(2,1)S(1)} %pack.1), channel_id=1, source_target_pairs={{0,1},{1,0},{2,3},{3,2},{4,5},{5,4},{6,7},{7,6},{8,9},{9,8},{10,11... | collective-permute-start | bytes 405512 | tf_op jit(solution)/shard_map/ppermute | solution.py:20
  4.7 1.5 %collective-permute-start = (bf16[528,128]{1,0:T(8,128)(2,1)S(1)}, bf16[528,128]{1,0:T(8,128)(2,1)S(1)}, u32[]{:S(2)}, u32[]{:S(2)}) collective-permute-start(bf16[528,128]{1,0:T(8,128)(2,1)S(1)} %pack.1), channel_id=1, source_target_pairs={{0,8},{1,9},{2,10},{3,11},{4,20},{5,21},{6,22},{7,23},{8,0},{9,1},... | collective-permute-start | bytes 405512 | tf_op jit(solution)/shard_map/ppermute | solution.py:20
  6.2 2.6 %collective-permute-start.3 = (bf16[528,128]{1,0:T(8,128)(2,1)S(1)}, bf16[528,128]{1,0:T(8,128)(2,1)S(1)}, u32[]{:S(2)}, u32[]{:S(2)}) collective-permute-start(bf16[528,128]{1,0:T(8,128)(2,1)S(1)} %pack.1), channel_id=1, source_target_pairs={{0,2},{1,3},{2,0},{3,1},{4,6},{5,7},{6,4},{7,5},{8,10},{9,11},{10,... | collective-permute-start | bytes 405512 | tf_op jit(solution)/shard_map/ppermute | solution.py:20
  8.8 0.0 collective-permute-done.2
  8.9 1.1 %collective-permute-start.7 = (bf16[528,128]{1,0:T(8,128)(2,1)S(1)}, bf16[528,128]{1,0:T(8,128)(2,1)S(1)}, u32[]{:S(2)}, u32[]{:S(2)}) collective-permute-start(bf16[528,128]{1,0:T(8,128)(2,1)S(1)} %collective-permute-done.2), channel_id=1, source_target_pairs={{0,8},{1,9},{2,10},{3,11},{4,20},{5,21},{6,22},{7,23},{8,0},{9,1},... | collective-permute-start | bytes 405512 | tf_op jit(solution)/shard_map/ppermute | solution.py:20
  10.0 3.2 %collective-permute-start.1 = (bf16[1056,128]{1,0:T(8,128)(2,1)S(1)}, bf16[1056,128]{1,0:T(8,128)(2,1)S(1)}, u32[]{:S(2)}, u32[]{:S(2)}) collective-permute-start(bf16[1056,128]{1,0:T(8,128)(2,1)S(1)} %pad_maximum_fusion), channel_id=1, source_target_pairs={{0,16},{1,17},{2,18},{3,19},{4,12},{5,13},{6,14},{7,15},{8,24},{9,... | collective-permute-start | bytes 811016 | tf_op jit(solution)/shard_map/ppermute | solution.py:20
  13.2 1.6 %collective-permute-done.3 = bf16[528,128]{1,0:T(8,128)(2,1)S(1)} collective-permute-done((bf16[528,128]{1,0:T(8,128)(2,1)S(1)}, bf16[528,128]{1,0:T(8,128)(2,1)S(1)}, u32[]{:S(2)}, u32[]{:S(2)}) %collective-permute-start.3) | collective-permute-done | bytes 135200 | tf_op jit(solution)/shard_map/ppermute | solution.py:20
  14.8 1.5 %collective-permute-start.4 = (bf16[528,128]{1,0:T(8,128)(2,1)S(1)}, bf16[528,128]{1,0:T(8,128)(2,1)S(1)}, u32[]{:S(2)}, u32[]{:S(2)}) collective-permute-start(bf16[528,128]{1,0:T(8,128)(2,1)S(1)} %collective-permute-done.3), channel_id=1, source_target_pairs={{0,8},{1,9},{2,10},{3,11},{4,20},{5,21},{6,22},{7,23},{8,0},{9,1},... | collective-permute-start | bytes 405512 | tf_op jit(solution)/shard_map/ppermute | solution.py:20
  16.3 0.6 %collective-permute-start.5 = (bf16[528,128]{1,0:T(8,128)(2,1)S(1)}, bf16[528,128]{1,0:T(8,128)(2,1)S(1)}, u32[]{:S(2)}, u32[]{:S(2)}) collective-permute-start(bf16[528,128]{1,0:T(8,128)(2,1)S(1)} %collective-permute-done.3), channel_id=1, source_target_pairs={{0,16},{1,17},{2,18},{3,19},{4,12},{5,13},{6,14},{7,15},{8,24},{9,... | collective-permute-start | bytes 405512 | tf_op jit(solution)/shard_map/ppermute | solution.py:20
  16.9 0.2 collective-permute-start.9
  17.1 1.3 %collective-permute-start.8 = (bf16[1056,128]{1,0:T(8,128)(2,1)S(1)}, bf16[1056,128]{1,0:T(8,128)(2,1)S(1)}, u32[]{:S(2)}, u32[]{:S(2)}) collective-permute-start(bf16[1056,128]{1,0:T(8,128)(2,1)S(1)} %pad_maximum_fusion.1), channel_id=1, source_target_pairs={{0,16},{1,17},{2,18},{3,19},{4,12},{5,13},{6,14},{7,15},{8,24},{9,... | collective-permute-start | bytes 811016 | tf_op jit(solution)/shard_map/ppermute | solution.py:20
  18.5 2.9 %collective-permute-done.5 = bf16[528,128]{1,0:T(8,128)(2,1)S(1)} collective-permute-done((bf16[528,128]{1,0:T(8,128)(2,1)S(1)}, bf16[528,128]{1,0:T(8,128)(2,1)S(1)}, u32[]{:S(2)}, u32[]{:S(2)}) %collective-permute-start.5) | collective-permute-done | bytes 135200 | tf_op jit(solution)/shard_map/ppermute | solution.py:20
  21.3 0.0 collective-permute-start.14
  21.3 0.0 collective-permute-done.4
  21.3 2.0 %collective-permute-start.12 = (bf16[528,128]{1,0:T(8,128)(2,1)S(1)}, bf16[528,128]{1,0:T(8,128)(2,1)S(1)}, u32[]{:S(2)}, u32[]{:S(2)}) collective-permute-start(bf16[528,128]{1,0:T(8,128)(2,1)S(1)} %collective-permute-done.4), channel_id=1, source_target_pairs={{0,1},{1,0},{2,3},{3,2},{4,5},{5,4},{6,7},{7,6},{8,9},{9,8},{10,11... | collective-permute-start | bytes 405512 | tf_op jit(solution)/shard_map/ppermute | solution.py:20
  23.3 0.0 collective-permute-done.1
  23.5 0.1 collective-permute-start.6
  23.7 1.1 %collective-permute-start.10 = (bf16[1056,128]{1,0:T(8,128)(2,1)S(1)}, bf16[1056,128]{1,0:T(8,128)(2,1)S(1)}, u32[]{:S(2)}, u32[]{:S(2)}) collective-permute-start(bf16[1056,128]{1,0:T(8,128)(2,1)S(1)} %pad_maximum_fusion.2), channel_id=1, source_target_pairs={{0,16},{1,17},{2,18},{3,19},{4,12},{5,13},{6,14},{7,15},{8,24},{9,... | collective-permute-start | bytes 811016 | tf_op jit(solution)/shard_map/ppermute | solution.py:20
  24.8 3.7 %collective-permute-done.12 = bf16[528,128]{1,0:T(8,128)(2,1)S(1)} collective-permute-done((bf16[528,128]{1,0:T(8,128)(2,1)S(1)}, bf16[528,128]{1,0:T(8,128)(2,1)S(1)}, u32[]{:S(2)}, u32[]{:S(2)}) %collective-permute-start.12) | collective-permute-done | bytes 135200 | tf_op jit(solution)/shard_map/ppermute | solution.py:20
  28.5 0.1 collective-permute-start.13
  28.6 0.1 collective-permute-done.14.refs_7_
  28.7 0.4 %collective-permute-start.15 = (bf16[528,128]{1,0:T(8,128)(2,1)S(1)}, bf16[528,128]{1,0:T(8,128)(2,1)S(1)}, u32[]{:S(2)}, u32[]{:S(2)}) collective-permute-start(bf16[528,128]{1,0:T(8,128)(2,1)S(1)} %collective-permute-done.14.refs_7_), channel_id=1, source_target_pairs={{0,4},{1,5},{2,6},{3,7},{4,0},{5,1},{6,2},{7,3},{8,12},{9,13},{10,... | collective-permute-start | bytes 405512 | tf_op jit(solution)/shard_map/ppermute | solution.py:20
  29.2 0.0 copy-start
  29.2 0.0 copy-start.1
  29.2 0.0 copy-start.2
  29.2 1.0 %collective-permute-done.10 = bf16[1056,128]{1,0:T(8,128)(2,1)S(1)} collective-permute-done((bf16[1056,128]{1,0:T(8,128)(2,1)S(1)}, bf16[1056,128]{1,0:T(8,128)(2,1)S(1)}, u32[]{:S(2)}, u32[]{:S(2)}) %collective-permute-start.10) | collective-permute-done | bytes 270368 | tf_op jit(solution)/shard_map/ppermute | solution.py:20
  30.2 0.4 collective-permute-start.11
  30.6 1.5 %sum_spans.1 = (f32[128,128]{1,0:T(8,128)S(1)}, f32[256,1024]{1,0:T(8,128)S(1)}) custom-call(bf16[128,1024]{1,0:T(8,128)(2,1)S(1)} %copy-done, s32[1,256]{1,0:T(1,128)S(1)} %copy-done.1, s32[128]{0:T(128)S(1)} %copy-done.2, bf16[3696,128]{1,0:T(8,128)(2,1)S(1)} %constant_dynamic-update-slice_fusion.refs_0_, bf16[3696,128]{1,0:T(8,128)(2,1)S(1)} %collective-permute-done.6.refs_1_), custom_call_target="tpu_custom_call" | custom-call | flops 10000000000 | tf_op jit(solution)/shard_map/sum_spans/pallas_call | solution.py:150
  32.1 0.1 collective-permute-done.11.refs_4_
  32.2 0.7 %copy-done.3 = f32[128]{0:T(128)S(1)} copy-done((f32[128]{0:T(128)S(1)}, f32[128]{0:T(128)}, u32[]{:S(2)}) %copy-start.3) | copy-done | bytes 536
  32.9 2.9 %close.1 = (f32[128,1024]{1,0:T(8,128)}, f32[128]{0:T(128)}) custom-call(bf16[128,1024]{1,0:T(8,128)(2,1)S(1)} %copy-done, s32[1,256]{1,0:T(1,128)S(1)} %copy-done.1, s32[128]{0:T(128)S(1)} %copy-done.2, f32[128]{0:T(128)S(1)} %copy-done.3, f32[128,128]{1,0:T(8,128)S(1)} %get-tuple-element.8.refs_1_, f32[256,1024]{1,0:T(8,128)S(1)} %get-tuple-element.9.refs_2_, ...), custom_call_target="tpu_custom_call" | custom-call | tf_op jit(solution)/shard_map/close/pallas_call | solution.py:150
  (26 shorter events, 0.3 us)
Async XLA Ops:
  1.7 7.2 %collective-permute-start.2 = (bf16[528,128]{1,0:T(8,128)(2,1)S(1)}, bf16[528,128]{1,0:T(8,128)(2,1)S(1)}, u32[]{:S(2)}, u32[]{:S(2)}) collective-permute-start(bf16[528,128]{1,0:T(8,128)(2,1)S(1)} %pack.1), channel_id=1, source_target_pairs={{0,1},{1,0},{2,3},{3,2},{4,5},{5,4},{6,7},{7,6},{8,9},{9,8},{10,11... | collective-permute-start | bytes 405512 | tf_op jit(solution)/shard_map/ppermute | solution.py:20
  4.7 5.2 %collective-permute-start = (bf16[528,128]{1,0:T(8,128)(2,1)S(1)}, bf16[528,128]{1,0:T(8,128)(2,1)S(1)}, u32[]{:S(2)}, u32[]{:S(2)}) collective-permute-start(bf16[528,128]{1,0:T(8,128)(2,1)S(1)} %pack.1), channel_id=1, source_target_pairs={{0,8},{1,9},{2,10},{3,11},{4,20},{5,21},{6,22},{7,23},{8,0},{9,1},... | collective-permute-start | bytes 405512 | tf_op jit(solution)/shard_map/ppermute | solution.py:20
  6.2 8.6 %collective-permute-start.3 = (bf16[528,128]{1,0:T(8,128)(2,1)S(1)}, bf16[528,128]{1,0:T(8,128)(2,1)S(1)}, u32[]{:S(2)}, u32[]{:S(2)}) collective-permute-start(bf16[528,128]{1,0:T(8,128)(2,1)S(1)} %pack.1), channel_id=1, source_target_pairs={{0,2},{1,3},{2,0},{3,1},{4,6},{5,7},{6,4},{7,5},{8,10},{9,11},{10,... | collective-permute-start | bytes 405512 | tf_op jit(solution)/shard_map/ppermute | solution.py:20
  8.9 8.3 %collective-permute-start.7 = (bf16[528,128]{1,0:T(8,128)(2,1)S(1)}, bf16[528,128]{1,0:T(8,128)(2,1)S(1)}, u32[]{:S(2)}, u32[]{:S(2)}) collective-permute-start(bf16[528,128]{1,0:T(8,128)(2,1)S(1)} %collective-permute-done.2), channel_id=1, source_target_pairs={{0,8},{1,9},{2,10},{3,11},{4,20},{5,21},{6,22},{7,23},{8,0},{9,1},... | collective-permute-start | bytes 405512 | tf_op jit(solution)/shard_map/ppermute | solution.py:20
  10.0 13.3 %collective-permute-start.1 = (bf16[1056,128]{1,0:T(8,128)(2,1)S(1)}, bf16[1056,128]{1,0:T(8,128)(2,1)S(1)}, u32[]{:S(2)}, u32[]{:S(2)}) collective-permute-start(bf16[1056,128]{1,0:T(8,128)(2,1)S(1)} %pad_maximum_fusion), channel_id=1, source_target_pairs={{0,16},{1,17},{2,18},{3,19},{4,12},{5,13},{6,14},{7,15},{8,24},{9,... | collective-permute-start | bytes 811016 | tf_op jit(solution)/shard_map/ppermute | solution.py:20
  14.8 6.5 %collective-permute-start.4 = (bf16[528,128]{1,0:T(8,128)(2,1)S(1)}, bf16[528,128]{1,0:T(8,128)(2,1)S(1)}, u32[]{:S(2)}, u32[]{:S(2)}) collective-permute-start(bf16[528,128]{1,0:T(8,128)(2,1)S(1)} %collective-permute-done.3), channel_id=1, source_target_pairs={{0,8},{1,9},{2,10},{3,11},{4,20},{5,21},{6,22},{7,23},{8,0},{9,1},... | collective-permute-start | bytes 405512 | tf_op jit(solution)/shard_map/ppermute | solution.py:20
  16.3 5.0 %collective-permute-start.5 = (bf16[528,128]{1,0:T(8,128)(2,1)S(1)}, bf16[528,128]{1,0:T(8,128)(2,1)S(1)}, u32[]{:S(2)}, u32[]{:S(2)}) collective-permute-start(bf16[528,128]{1,0:T(8,128)(2,1)S(1)} %collective-permute-done.3), channel_id=1, source_target_pairs={{0,16},{1,17},{2,18},{3,19},{4,12},{5,13},{6,14},{7,15},{8,24},{9,... | collective-permute-start | bytes 405512 | tf_op jit(solution)/shard_map/ppermute | solution.py:20
  16.9 6.7 %collective-permute-start.9 = (bf16[528,128]{1,0:T(8,128)(2,1)S(1)}, bf16[528,128]{1,0:T(8,128)(2,1)S(1)}, u32[]{:S(2)}, u32[]{:S(2)}) collective-permute-start(bf16[528,128]{1,0:T(8,128)(2,1)S(1)} %collective-permute-done.3), channel_id=1, source_target_pairs={{0,1},{1,0},{2,3},{3,2},{4,5},{5,4},{6,7},{7,6},{8,9},{9,8},{10,11... | collective-permute-start | bytes 405512 | tf_op jit(solution)/shard_map/ppermute | solution.py:20
  17.1 12.0 %collective-permute-start.8 = (bf16[1056,128]{1,0:T(8,128)(2,1)S(1)}, bf16[1056,128]{1,0:T(8,128)(2,1)S(1)}, u32[]{:S(2)}, u32[]{:S(2)}) collective-permute-start(bf16[1056,128]{1,0:T(8,128)(2,1)S(1)} %pad_maximum_fusion.1), channel_id=1, source_target_pairs={{0,16},{1,17},{2,18},{3,19},{4,12},{5,13},{6,14},{7,15},{8,24},{9,... | collective-permute-start | bytes 811016 | tf_op jit(solution)/shard_map/ppermute | solution.py:20
  21.3 7.4 %collective-permute-start.14 = (bf16[528,128]{1,0:T(8,128)(2,1)S(1)}, bf16[528,128]{1,0:T(8,128)(2,1)S(1)}, u32[]{:S(2)}, u32[]{:S(2)}) collective-permute-start(bf16[528,128]{1,0:T(8,128)(2,1)S(1)} %collective-permute-done.5), channel_id=1, source_target_pairs={{0,9},{1,8},{2,11},{3,10},{4,21},{5,20},{6,23},{7,22},{8,1},{9,0},... | collective-permute-start | bytes 405512 | tf_op jit(solution)/shard_map/ppermute | solution.py:20
  21.3 7.2 %collective-permute-start.12 = (bf16[528,128]{1,0:T(8,128)(2,1)S(1)}, bf16[528,128]{1,0:T(8,128)(2,1)S(1)}, u32[]{:S(2)}, u32[]{:S(2)}) collective-permute-start(bf16[528,128]{1,0:T(8,128)(2,1)S(1)} %collective-permute-done.4), channel_id=1, source_target_pairs={{0,1},{1,0},{2,3},{3,2},{4,5},{5,4},{6,7},{7,6},{8,9},{9,8},{10,11... | collective-permute-start | bytes 405512 | tf_op jit(solution)/shard_map/ppermute | solution.py:20
  23.5 7.1 %collective-permute-start.6 = (bf16[3696,128]{1,0:T(8,128)(2,1)S(1)}, bf16[3696,128]{1,0:T(8,128)(2,1)S(1)}, u32[]{:S(2)}, u32[]{:S(2)}) collective-permute-start(bf16[3696,128]{1,0:T(8,128)(2,1)S(1)} %constant_dynamic-update-slice_fusion.refs_0_), channel_id=1, source_target_pairs={{0,4},{1,5},{2,6},{3,7},{4,0},{5,1},{6,2},{7,3},{8,12},{9,13},{10,... | collective-permute-start | bytes 2838536 | tf_op jit(solution)/shard_map/ppermute | solution.py:20
  23.7 6.5 %collective-permute-start.10 = (bf16[1056,128]{1,0:T(8,128)(2,1)S(1)}, bf16[1056,128]{1,0:T(8,128)(2,1)S(1)}, u32[]{:S(2)}, u32[]{:S(2)}) collective-permute-start(bf16[1056,128]{1,0:T(8,128)(2,1)S(1)} %pad_maximum_fusion.2), channel_id=1, source_target_pairs={{0,16},{1,17},{2,18},{3,19},{4,12},{5,13},{6,14},{7,15},{8,24},{9,... | collective-permute-start | bytes 811016 | tf_op jit(solution)/shard_map/ppermute | solution.py:20
  28.5 3.6 %collective-permute-start.13 = (bf16[2112,128]{1,0:T(8,128)(2,1)S(1)}, bf16[2112,128]{1,0:T(8,128)(2,1)S(1)}, u32[]{:S(2)}, u32[]{:S(2)}) collective-permute-start(bf16[2112,128]{1,0:T(8,128)(2,1)S(1)} %constant_dynamic-update-slice_fusion.8.refs_5_), channel_id=1, source_target_pairs={{0,4},{1,5},{2,6},{3,7},{4,0},{5,1},{6,2},{7,3},{8,12},{9,13},{10,... | collective-permute-start | bytes 1622024 | tf_op jit(solution)/shard_map/ppermute | solution.py:20
  28.7 3.4 %collective-permute-start.15 = (bf16[528,128]{1,0:T(8,128)(2,1)S(1)}, bf16[528,128]{1,0:T(8,128)(2,1)S(1)}, u32[]{:S(2)}, u32[]{:S(2)}) collective-permute-start(bf16[528,128]{1,0:T(8,128)(2,1)S(1)} %collective-permute-done.14.refs_7_), channel_id=1, source_target_pairs={{0,4},{1,5},{2,6},{3,7},{4,0},{5,1},{6,2},{7,3},{8,12},{9,13},{10,... | collective-permute-start | bytes 405512 | tf_op jit(solution)/shard_map/ppermute | solution.py:20
  29.2 1.4 %copy-start = (bf16[128,1024]{1,0:T(8,128)(2,1)S(1)}, bf16[128,1024]{1,0:T(8,128)(2,1)}, u32[]{:S(2)}) copy-start(bf16[128,1024]{1,0:T(8,128)(2,1)} %queries_ref.3) | copy-start | bytes 786436
  29.2 1.4 %copy-start.1 = (s32[1,256]{1,0:T(1,128)S(1)}, s32[1,256]{1,0:T(1,128)}, u32[]{:S(2)}) copy-start(s32[1,256]{1,0:T(1,128)} %pattern_ref.3) | copy-start | bytes 3076
  29.2 1.4 %copy-start.2 = (s32[128]{0:T(128)S(1)}, s32[128]{0:T(128)}, u32[]{:S(2)}) copy-start(s32[128]{0:T(128)} %positives_ref.3) | copy-start | bytes 1540
  30.2 2.0 %collective-permute-start.11 = (bf16[2112,128]{1,0:T(8,128)(2,1)S(1)}, bf16[2112,128]{1,0:T(8,128)(2,1)S(1)}, u32[]{:S(2)}, u32[]{:S(2)}) collective-permute-start(bf16[2112,128]{1,0:T(8,128)(2,1)S(1)} %constant_dynamic-update-slice_fusion.6.refs_3_), channel_id=1, source_target_pairs={{0,4},{1,5},{2,6},{3,7},{4,0},{5,1},{6,2},{7,3},{8,12},{9,13},{10,... | collective-permute-start | bytes 1622024 | tf_op jit(solution)/shard_map/ppermute | solution.py:20
  32.2 0.7 %copy-start.3 = (f32[128]{0:T(128)S(1)}, f32[128]{0:T(128)}, u32[]{:S(2)}) copy-start(f32[128]{0:T(128)} %refs_0_.1) | copy-start | bytes 1540

commit v3 on v2

--- a/solution.py
+++ b/solution.py
@@ -172,9 +172,12 @@
     def join(values):
         return values[0] if len(values) == 1 else jnp.concatenate(values, axis=0)
 
-    def both(values):
+    def after(value, *earlier):
+        return lax.optimization_barrier((value, *earlier))[0] if earlier else value
+
+    def both(values, *earlier):
         value = join(values)
-        return [value, along(value, core)]
+        return [value, along(after(value, *earlier), core)]
 
     own = pack(keys, clusters)
     unit = own.shape[0]
@@ -188,24 +191,21 @@
         flips = [sum(1 << place for bit, place in bits.items() if way & bit) for way in ways]
         return exchange(value, counts, lambda i: i ^ flips[(i >> core) & 1])
 
-    def after(value, *earlier):
-        return lax.optimization_barrier((value, *earlier))[0]
-
     v0 = own
     v1 = go(v0, 1, 2)
-    v2_3 = go(join([v0, v1]), 2, 1)
-    v4 = go(v0, 4, 4)
+    v2_3 = go(join([v0, v1]), 2, 4)
+    v4 = go(v0, 4, 1)
     v5 = go(v4, 1, 2)
-    v6_7 = go(join([v4, v5]), 2, 1)
+    v6_7 = go(join([v4, v5]), 2, 4)
     v8 = go(v0, 8, 8)
     v9 = go(after(v8, v4), 1, 2)
-    v10 = go(v8, 2, 1)
-    v12 = go(v8, 4, 4)
-    v14_11 = go(after(join([v12, v9]), v2_3), 2, 1)
-    v13 = go(v9, 4, 4)
-    v15 = go(after(v10, v10), 5, 6)
-    part = sum_spans(*args, both([v0, v2_3, v4, v8, v9, v10]), cost=int(10000000000.0))
-    return sum_spans(*args, both([v6_7, v14_11]) + both([v1, v5, v12, v13]) + both([v15]), loss_multiplier, [part])
+    v10 = go(v8, 2, 4)
+    v12 = go(v8, 4, 1)
+    v14_11 = go(after(join([v12, v9]), v2_3), 2, 4)
+    v13 = go(after(v9, v4), 4, 1)
+    v15 = go(v10, 5, 3)
+    part = sum_spans(*args, both([v0, v1, v2_3, v4, v5, v8, v9]) + both([v6_7[0*unit:1*unit], v10, v12]), cost=int(4000000000.0))
+    return sum_spans(*args, both([v6_7[1*unit:2*unit], v14_11, v13, v15]), loss_multiplier, [part])
 
 
 def doubling(counts, args, own, loss_multiplier):

time: 35.9 us -> 34.5 us (0.961)
  starting transfers between devices: 19.2 us -> 18.1 us
  local copies, waits for them, and re-layouts: 0.92 us -> 0.19 us
  waiting for transfers between devices: 9.4 us -> 9.82 us
    ppermute x16 -> x15, starting transfers between devices: 19.2 us -> 18.1 us  [exchange(): return lax.ppermute(value, AXES, [(i, flip(i)) for i in range(total)])]
    unnamed x17 -> x14, local copies, waits for them, and re-layouts: 0.85 us -> 0.15 us
    ppermute x16 -> x15, waiting for transfers between devices: 9.4 us -> 9.82 us  [exchange(): return lax.ppermute(value, AXES, [(i, flip(i)) for i in range(total)])]
  transfers between devices with their start and end apart: 16 -> 15, of which waited for: 6 -> 6; matrix products, arithmetic and copies ran while one was open for 1% -> 1% of each run, Pallas kernels for 4% -> 6%
where the time goes in v3:
time: 34.5 us; the launch traced here: 34.4 us
  starting transfers between devices  18.1 us (52%)
  waiting for transfers between devices  9.82 us (28%)
  Pallas kernels  5.29 us (15%)
  between operations  0.84 us (2%)
    ppermute x15, starting transfers between devices, exchange(): return lax.ppermute(value, AXES, [(i, flip(i)) for i in range(total)])  18.1 us
    ppermute x15, waiting for transfers between devices, exchange(): return lax.ppermute(value, AXES, [(i, flip(i)) for i in range(total)])  9.82 us
    pallas_call x2, Pallas kernels, sum_spans(): pl.pallas_call(functools.partial(sum_kernel, rows, group, closing, len(pr...  4.27 us
    pallas_call x1, Pallas kernels, pack(): pl.pallas_call(pack_kernel, out_shape=pltpu.VMEM((width // LANES * rows +...  1.02 us
  transfers between devices with their start and end apart: 15, of which 6 were waited for; matrix products, arithmetic and copies ran while one was open for 1% of the time, Pallas kernels for 6%

profile of v3, /device:TPU:0, one launch (start us, length us, event | category | flops | bytes accessed | tf_op | source)
XLA Modules:
  0.0 34.4 jit_solution(9534151160319894867)
XLA Ops:
  0.6 1.0 %pack.1 = bf16[528,128]{1,0:T(8,128)(2,1)S(1)} custom-call(bf16[64,1024]{1,0:T(8,128)(2,1)} %keys_ref.1, s32[64]{0:T(128)} %clusters_ref.1), custom_call_target="tpu_custom_call" | custom-call | tf_op jit(solution)/shard_map/pack/pallas_call | solution.py:43
  1.7 3.1 %collective-permute-start.2 = (bf16[528,128]{1,0:T(8,128)(2,1)S(1)}, bf16[528,128]{1,0:T(8,128)(2,1)S(1)}, u32[]{:S(2)}, u32[]{:S(2)}) collective-permute-start(bf16[528,128]{1,0:T(8,128)(2,1)S(1)} %pack.1), channel_id=1, source_target_pairs={{0,1},{1,0},{2,3},{3,2},{4,12},{5,13},{6,14},{7,15},{8,9},{9,8},{1... | collective-permute-start | bytes 405512 | tf_op jit(solution)/shard_map/ppermute | solution.py:20
  4.7 1.5 %collective-permute-start = (bf16[528,128]{1,0:T(8,128)(2,1)S(1)}, bf16[528,128]{1,0:T(8,128)(2,1)S(1)}, u32[]{:S(2)}, u32[]{:S(2)}) collective-permute-start(bf16[528,128]{1,0:T(8,128)(2,1)S(1)} %pack.1), channel_id=1, source_target_pairs={{0,8},{1,9},{2,10},{3,11},{4,20},{5,21},{6,22},{7,23},{8,0},{9,1},... | collective-permute-start | bytes 405512 | tf_op jit(solution)/shard_map/ppermute | solution.py:20
  6.2 2.6 %collective-permute-start.4 = (bf16[528,128]{1,0:T(8,128)(2,1)S(1)}, bf16[528,128]{1,0:T(8,128)(2,1)S(1)}, u32[]{:S(2)}, u32[]{:S(2)}) collective-permute-start(bf16[528,128]{1,0:T(8,128)(2,1)S(1)} %pack.1), channel_id=1, source_target_pairs={{0,2},{1,3},{2,0},{3,1},{4,6},{5,7},{6,4},{7,5},{8,10},{9,11},{10,... | collective-permute-start | bytes 405512 | tf_op jit(solution)/shard_map/ppermute | solution.py:20
  8.8 0.0 collective-permute-done.2
  8.9 1.9 %collective-permute-start.3 = (bf16[528,128]{1,0:T(8,128)(2,1)S(1)}, bf16[528,128]{1,0:T(8,128)(2,1)S(1)}, u32[]{:S(2)}, u32[]{:S(2)}) collective-permute-start(bf16[528,128]{1,0:T(8,128)(2,1)S(1)} %collective-permute-done.2), channel_id=1, source_target_pairs={{0,8},{1,9},{2,10},{3,11},{4,20},{5,21},{6,22},{7,23},{8,0},{9,1},... | collective-permute-start | bytes 405512 | tf_op jit(solution)/shard_map/ppermute | solution.py:20
  10.8 1.9 %collective-permute-start.1 = (bf16[1056,128]{1,0:T(8,128)(2,1)S(1)}, bf16[1056,128]{1,0:T(8,128)(2,1)S(1)}, u32[]{:S(2)}, u32[]{:S(2)}) collective-permute-start(bf16[1056,128]{1,0:T(8,128)(2,1)S(1)} %pad_maximum_fusion.2), channel_id=1, source_target_pairs={{0,16},{1,17},{2,18},{3,19},{4,5},{5,4},{6,7},{7,6},{8,24},{9,25},... | collective-permute-start | bytes 811016 | tf_op jit(solution)/shard_map/ppermute | solution.py:20
  12.7 2.1 %collective-permute-done.4 = bf16[528,128]{1,0:T(8,128)(2,1)S(1)} collective-permute-done((bf16[528,128]{1,0:T(8,128)(2,1)S(1)}, bf16[528,128]{1,0:T(8,128)(2,1)S(1)}, u32[]{:S(2)}, u32[]{:S(2)}) %collective-permute-start.4) | collective-permute-done | bytes 135200 | tf_op jit(solution)/shard_map/ppermute | solution.py:20
  14.9 0.6 %collective-permute-start.5 = (bf16[528,128]{1,0:T(8,128)(2,1)S(1)}, bf16[528,128]{1,0:T(8,128)(2,1)S(1)}, u32[]{:S(2)}, u32[]{:S(2)}) collective-permute-start(bf16[528,128]{1,0:T(8,128)(2,1)S(1)} %collective-permute-done.4), channel_id=1, source_target_pairs={{0,8},{1,9},{2,10},{3,11},{4,20},{5,21},{6,22},{7,23},{8,0},{9,1},... | collective-permute-start | bytes 405512 | tf_op jit(solution)/shard_map/ppermute | solution.py:20
  15.4 0.5 %collective-permute-start.8 = (bf16[528,128]{1,0:T(8,128)(2,1)S(1)}, bf16[528,128]{1,0:T(8,128)(2,1)S(1)}, u32[]{:S(2)}, u32[]{:S(2)}) collective-permute-start(bf16[528,128]{1,0:T(8,128)(2,1)S(1)} %collective-permute-done.4), channel_id=1, source_target_pairs={{0,16},{1,17},{2,18},{3,19},{4,5},{5,4},{6,7},{7,6},{8,24},{9,25},... | collective-permute-start | bytes 405512 | tf_op jit(solution)/shard_map/ppermute | solution.py:20
  16.0 0.5 %collective-permute-start.9 = (bf16[528,128]{1,0:T(8,128)(2,1)S(1)}, bf16[528,128]{1,0:T(8,128)(2,1)S(1)}, u32[]{:S(2)}, u32[]{:S(2)}) collective-permute-start(bf16[528,128]{1,0:T(8,128)(2,1)S(1)} %collective-permute-done.4), channel_id=1, source_target_pairs={{0,1},{1,0},{2,3},{3,2},{4,12},{5,13},{6,14},{7,15},{8,9},{9,8},{1... | collective-permute-start | bytes 405512 | tf_op jit(solution)/shard_map/ppermute | solution.py:20
  16.6 1.7 %collective-permute-start.7 = (bf16[1056,128]{1,0:T(8,128)(2,1)S(1)}, bf16[1056,128]{1,0:T(8,128)(2,1)S(1)}, u32[]{:S(2)}, u32[]{:S(2)}) collective-permute-start(bf16[1056,128]{1,0:T(8,128)(2,1)S(1)} %pad_maximum_fusion.3), channel_id=1, source_target_pairs={{0,16},{1,17},{2,18},{3,19},{4,5},{5,4},{6,7},{7,6},{8,24},{9,25},... | collective-permute-start | bytes 811016 | tf_op jit(solution)/shard_map/ppermute | solution.py:20
  18.2 2.5 %collective-permute-done.5 = bf16[528,128]{1,0:T(8,128)(2,1)S(1)} collective-permute-done((bf16[528,128]{1,0:T(8,128)(2,1)S(1)}, bf16[528,128]{1,0:T(8,128)(2,1)S(1)}, u32[]{:S(2)}, u32[]{:S(2)}) %collective-permute-start.5) | collective-permute-done | bytes 135200 | tf_op jit(solution)/shard_map/ppermute | solution.py:20
  20.7 0.3 collective-permute-start.12
  21.0 0.0 collective-permute-done.8
  21.0 1.8 %collective-permute-start.13 = (bf16[528,128]{1,0:T(8,128)(2,1)S(1)}, bf16[528,128]{1,0:T(8,128)(2,1)S(1)}, u32[]{:S(2)}, u32[]{:S(2)}) collective-permute-start(bf16[528,128]{1,0:T(8,128)(2,1)S(1)} %collective-permute-done.8), channel_id=1, source_target_pairs={{0,9},{1,8},{2,11},{3,10},{4,28},{5,29},{6,30},{7,31},{8,1},{9,0},... | collective-permute-start | bytes 405512 | tf_op jit(solution)/shard_map/ppermute | solution.py:20
  22.8 0.0 collective-permute-done.9
  23.0 0.1 collective-permute-start.6
  23.1 1.1 %collective-permute-start.11 = (bf16[1056,128]{1,0:T(8,128)(2,1)S(1)}, bf16[1056,128]{1,0:T(8,128)(2,1)S(1)}, u32[]{:S(2)}, u32[]{:S(2)}) collective-permute-start(bf16[1056,128]{1,0:T(8,128)(2,1)S(1)} %pad_maximum_fusion.4), channel_id=1, source_target_pairs={{0,16},{1,17},{2,18},{3,19},{4,5},{5,4},{6,7},{7,6},{8,24},{9,25},... | collective-permute-start | bytes 811016 | tf_op jit(solution)/shard_map/ppermute | solution.py:20
  24.2 0.5 %collective-permute-done.7 = bf16[1056,128]{1,0:T(8,128)(2,1)S(1)} collective-permute-done((bf16[1056,128]{1,0:T(8,128)(2,1)S(1)}, bf16[1056,128]{1,0:T(8,128)(2,1)S(1)}, u32[]{:S(2)}, u32[]{:S(2)}) %collective-permute-start.7) | collective-permute-done | bytes 270368 | tf_op jit(solution)/shard_map/ppermute | solution.py:20
  24.8 0.0 copy-start
  24.8 0.0 copy-start.1
  24.8 0.0 copy-start.2
  24.9 0.1 collective-permute-start.10
  25.0 0.8 %collective-permute-done.12 = bf16[528,128]{1,0:T(8,128)(2,1)S(1)} collective-permute-done((bf16[528,128]{1,0:T(8,128)(2,1)S(1)}, bf16[528,128]{1,0:T(8,128)(2,1)S(1)}, u32[]{:S(2)}, u32[]{:S(2)}) %collective-permute-start.12) | collective-permute-done | bytes 135200 | tf_op jit(solution)/shard_map/ppermute | solution.py:20
  25.7 1.7 %collective-permute-done.13 = bf16[528,128]{1,0:T(8,128)(2,1)S(1)} collective-permute-done((bf16[528,128]{1,0:T(8,128)(2,1)S(1)}, bf16[528,128]{1,0:T(8,128)(2,1)S(1)}, u32[]{:S(2)}, u32[]{:S(2)}) %collective-permute-start.13) | collective-permute-done | bytes 135200 | tf_op jit(solution)/shard_map/ppermute | solution.py:20
  27.4 2.2 %collective-permute-done.11 = bf16[1056,128]{1,0:T(8,128)(2,1)S(1)} collective-permute-done((bf16[1056,128]{1,0:T(8,128)(2,1)S(1)}, bf16[1056,128]{1,0:T(8,128)(2,1)S(1)}, u32[]{:S(2)}, u32[]{:S(2)}) %collective-permute-start.11) | collective-permute-done | bytes 270368 | tf_op jit(solution)/shard_map/ppermute | solution.py:20
  29.7 0.0 copy-start.3
  29.7 0.3 %collective-permute-start.14 = (bf16[2640,128]{1,0:T(8,128)(2,1)S(1)}, bf16[2640,128]{1,0:T(8,128)(2,1)S(1)}, u32[]{:S(2)}, u32[]{:S(2)}) collective-permute-start(bf16[2640,128]{1,0:T(8,128)(2,1)S(1)} %pad_maximum_fusion.refs_3_), channel_id=1, source_target_pairs={{0,4},{1,5},{2,6},{3,7},{4,0},{5,1},{6,2},{7,3},{8,12},{9,13},{10,... | collective-permute-start | bytes 2027528 | tf_op jit(solution)/shard_map/ppermute | solution.py:20
  30.0 0.0 collective-permute-done.10.refs_3_
  30.1 2.2 %sum_spans.1 = (f32[128,128]{1,0:T(8,128)S(1)}, f32[256,1024]{1,0:T(8,128)S(1)}) custom-call(bf16[128,1024]{1,0:T(8,128)(2,1)S(1)} %copy-done, s32[1,256]{1,0:T(1,128)S(1)} %copy-done.1, s32[128]{0:T(128)S(1)} %copy-done.2, bf16[4224,128]{1,0:T(8,128)(2,1)S(1)} %constant_dynamic-update-slice_fusion.refs_0_, ...), custom_call_target="tpu_custom_call" | custom-call | flops 4000000000 | tf_op jit(solution)/shard_map/sum_spans/pallas_call | solution.py:150
  32.3 2.1 %close.1 = (f32[128,1024]{1,0:T(8,128)}, f32[128]{0:T(128)}) custom-call(bf16[128,1024]{1,0:T(8,128)(2,1)S(1)} %copy-done, s32[1,256]{1,0:T(1,128)S(1)} %copy-done.1, s32[128]{0:T(128)S(1)} %copy-done.2, f32[128]{0:T(128)S(1)} %copy-done.3, f32[128,128]{1,0:T(8,128)S(1)} %get-tuple-element.8.refs_1_, f32[256,1024]{1,0:T(8,128)S(1)} %get-tuple-element.9.refs_2_, ...), custom_call_target="tpu_custom_call" | custom-call | tf_op jit(solution)/shard_map/close/pallas_call | solution.py:150
  (22 shorter events, 0.3 us)
Async XLA Ops:
  1.7 7.2 %collective-permute-start.2 = (bf16[528,128]{1,0:T(8,128)(2,1)S(1)}, bf16[528,128]{1,0:T(8,128)(2,1)S(1)}, u32[]{:S(2)}, u32[]{:S(2)}) collective-permute-start(bf16[528,128]{1,0:T(8,128)(2,1)S(1)} %pack.1), channel_id=1, source_target_pairs={{0,1},{1,0},{2,3},{3,2},{4,12},{5,13},{6,14},{7,15},{8,9},{9,8},{1... | collective-permute-start | bytes 405512 | tf_op jit(solution)/shard_map/ppermute | solution.py:20
  4.7 6.0 %collective-permute-start = (bf16[528,128]{1,0:T(8,128)(2,1)S(1)}, bf16[528,128]{1,0:T(8,128)(2,1)S(1)}, u32[]{:S(2)}, u32[]{:S(2)}) collective-permute-start(bf16[528,128]{1,0:T(8,128)(2,1)S(1)} %pack.1), channel_id=1, source_target_pairs={{0,8},{1,9},{2,10},{3,11},{4,20},{5,21},{6,22},{7,23},{8,0},{9,1},... | collective-permute-start | bytes 405512 | tf_op jit(solution)/shard_map/ppermute | solution.py:20
  6.2 8.6 %collective-permute-start.4 = (bf16[528,128]{1,0:T(8,128)(2,1)S(1)}, bf16[528,128]{1,0:T(8,128)(2,1)S(1)}, u32[]{:S(2)}, u32[]{:S(2)}) collective-permute-start(bf16[528,128]{1,0:T(8,128)(2,1)S(1)} %pack.1), channel_id=1, source_target_pairs={{0,2},{1,3},{2,0},{3,1},{4,6},{5,7},{6,4},{7,5},{8,10},{9,11},{10,... | collective-permute-start | bytes 405512 | tf_op jit(solution)/shard_map/ppermute | solution.py:20
  8.9 7.7 %collective-permute-start.3 = (bf16[528,128]{1,0:T(8,128)(2,1)S(1)}, bf16[528,128]{1,0:T(8,128)(2,1)S(1)}, u32[]{:S(2)}, u32[]{:S(2)}) collective-permute-start(bf16[528,128]{1,0:T(8,128)(2,1)S(1)} %collective-permute-done.2), channel_id=1, source_target_pairs={{0,8},{1,9},{2,10},{3,11},{4,20},{5,21},{6,22},{7,23},{8,0},{9,1},... | collective-permute-start | bytes 405512 | tf_op jit(solution)/shard_map/ppermute | solution.py:20
  10.8 12.0 %collective-permute-start.1 = (bf16[1056,128]{1,0:T(8,128)(2,1)S(1)}, bf16[1056,128]{1,0:T(8,128)(2,1)S(1)}, u32[]{:S(2)}, u32[]{:S(2)}) collective-permute-start(bf16[1056,128]{1,0:T(8,128)(2,1)S(1)} %pad_maximum_fusion.2), channel_id=1, source_target_pairs={{0,16},{1,17},{2,18},{3,19},{4,5},{5,4},{6,7},{7,6},{8,24},{9,25},... | collective-permute-start | bytes 811016 | tf_op jit(solution)/shard_map/ppermute | solution.py:20
  14.9 5.9 %collective-permute-start.5 = (bf16[528,128]{1,0:T(8,128)(2,1)S(1)}, bf16[528,128]{1,0:T(8,128)(2,1)S(1)}, u32[]{:S(2)}, u32[]{:S(2)}) collective-permute-start(bf16[528,128]{1,0:T(8,128)(2,1)S(1)} %collective-permute-done.4), channel_id=1, source_target_pairs={{0,8},{1,9},{2,10},{3,11},{4,20},{5,21},{6,22},{7,23},{8,0},{9,1},... | collective-permute-start | bytes 405512 | tf_op jit(solution)/shard_map/ppermute | solution.py:20
  15.4 5.6 %collective-permute-start.8 = (bf16[528,128]{1,0:T(8,128)(2,1)S(1)}, bf16[528,128]{1,0:T(8,128)(2,1)S(1)}, u32[]{:S(2)}, u32[]{:S(2)}) collective-permute-start(bf16[528,128]{1,0:T(8,128)(2,1)S(1)} %collective-permute-done.4), channel_id=1, source_target_pairs={{0,16},{1,17},{2,18},{3,19},{4,5},{5,4},{6,7},{7,6},{8,24},{9,25},... | collective-permute-start | bytes 405512 | tf_op jit(solution)/shard_map/ppermute | solution.py:20
  16.0 6.9 %collective-permute-start.9 = (bf16[528,128]{1,0:T(8,128)(2,1)S(1)}, bf16[528,128]{1,0:T(8,128)(2,1)S(1)}, u32[]{:S(2)}, u32[]{:S(2)}) collective-permute-start(bf16[528,128]{1,0:T(8,128)(2,1)S(1)} %collective-permute-done.4), channel_id=1, source_target_pairs={{0,1},{1,0},{2,3},{3,2},{4,12},{5,13},{6,14},{7,15},{8,9},{9,8},{1... | collective-permute-start | bytes 405512 | tf_op jit(solution)/shard_map/ppermute | solution.py:20
  16.6 8.2 %collective-permute-start.7 = (bf16[1056,128]{1,0:T(8,128)(2,1)S(1)}, bf16[1056,128]{1,0:T(8,128)(2,1)S(1)}, u32[]{:S(2)}, u32[]{:S(2)}) collective-permute-start(bf16[1056,128]{1,0:T(8,128)(2,1)S(1)} %pad_maximum_fusion.3), channel_id=1, source_target_pairs={{0,16},{1,17},{2,18},{3,19},{4,5},{5,4},{6,7},{7,6},{8,24},{9,25},... | collective-permute-start | bytes 811016 | tf_op jit(solution)/shard_map/ppermute | solution.py:20
  20.7 5.0 %collective-permute-start.12 = (bf16[528,128]{1,0:T(8,128)(2,1)S(1)}, bf16[528,128]{1,0:T(8,128)(2,1)S(1)}, u32[]{:S(2)}, u32[]{:S(2)}) collective-permute-start(bf16[528,128]{1,0:T(8,128)(2,1)S(1)} %collective-permute-done.5), channel_id=1, source_target_pairs={{0,1},{1,0},{2,3},{3,2},{4,12},{5,13},{6,14},{7,15},{8,9},{9,8},{1... | collective-permute-start | bytes 405512 | tf_op jit(solution)/shard_map/ppermute | solution.py:20
  21.0 6.4 %collective-permute-start.13 = (bf16[528,128]{1,0:T(8,128)(2,1)S(1)}, bf16[528,128]{1,0:T(8,128)(2,1)S(1)}, u32[]{:S(2)}, u32[]{:S(2)}) collective-permute-start(bf16[528,128]{1,0:T(8,128)(2,1)S(1)} %collective-permute-done.8), channel_id=1, source_target_pairs={{0,9},{1,8},{2,11},{3,10},{4,28},{5,29},{6,30},{7,31},{8,1},{9,0},... | collective-permute-start | bytes 405512 | tf_op jit(solution)/shard_map/ppermute | solution.py:20
  23.0 7.0 %collective-permute-start.6 = (bf16[4224,128]{1,0:T(8,128)(2,1)S(1)}, bf16[4224,128]{1,0:T(8,128)(2,1)S(1)}, u32[]{:S(2)}, u32[]{:S(2)}) collective-permute-start(bf16[4224,128]{1,0:T(8,128)(2,1)S(1)} %constant_dynamic-update-slice_fusion.refs_0_), channel_id=1, source_target_pairs={{0,4},{1,5},{2,6},{3,7},{4,0},{5,1},{6,2},{7,3},{8,12},{9,13},{10,... | collective-permute-start | bytes 3244040 | tf_op jit(solution)/shard_map/ppermute | solution.py:20
  23.1 6.5 %collective-permute-start.11 = (bf16[1056,128]{1,0:T(8,128)(2,1)S(1)}, bf16[1056,128]{1,0:T(8,128)(2,1)S(1)}, u32[]{:S(2)}, u32[]{:S(2)}) collective-permute-start(bf16[1056,128]{1,0:T(8,128)(2,1)S(1)} %pad_maximum_fusion.4), channel_id=1, source_target_pairs={{0,16},{1,17},{2,18},{3,19},{4,5},{5,4},{6,7},{7,6},{8,24},{9,25},... | collective-permute-start | bytes 811016 | tf_op jit(solution)/shard_map/ppermute | solution.py:20
  24.8 5.2 %copy-start = (bf16[128,1024]{1,0:T(8,128)(2,1)S(1)}, bf16[128,1024]{1,0:T(8,128)(2,1)}, u32[]{:S(2)}) copy-start(bf16[128,1024]{1,0:T(8,128)(2,1)} %queries_ref.3) | copy-start | bytes 786436
  24.8 5.2 %copy-start.1 = (s32[1,256]{1,0:T(1,128)S(1)}, s32[1,256]{1,0:T(1,128)}, u32[]{:S(2)}) copy-start(s32[1,256]{1,0:T(1,128)} %pattern_ref.3) | copy-start | bytes 3076
  24.8 5.2 %copy-start.2 = (s32[128]{0:T(128)S(1)}, s32[128]{0:T(128)}, u32[]{:S(2)}) copy-start(s32[128]{0:T(128)} %positives_ref.3) | copy-start | bytes 1540
  24.9 5.2 %collective-permute-start.10 = (bf16[1584,128]{1,0:T(8,128)(2,1)S(1)}, bf16[1584,128]{1,0:T(8,128)(2,1)S(1)}, u32[]{:S(2)}, u32[]{:S(2)}) collective-permute-start(bf16[1584,128]{1,0:T(8,128)(2,1)S(1)} %pad_maximum_fusion.1.refs_2_), channel_id=1, source_target_pairs={{0,4},{1,5},{2,6},{3,7},{4,0},{5,1},{6,2},{7,3},{8,12},{9,13},{10,... | collective-permute-start | bytes 1216520 | tf_op jit(solution)/shard_map/ppermute | solution.py:20
  29.7 2.6 %copy-start.3 = (f32[128]{0:T(128)S(1)}, f32[128]{0:T(128)}, u32[]{:S(2)}) copy-start(f32[128]{0:T(128)} %refs_0_.1) | copy-start | bytes 1540
  29.7 2.6 %collective-permute-start.14 = (bf16[2640,128]{1,0:T(8,128)(2,1)S(1)}, bf16[2640,128]{1,0:T(8,128)(2,1)S(1)}, u32[]{:S(2)}, u32[]{:S(2)}) collective-permute-start(bf16[2640,128]{1,0:T(8,128)(2,1)S(1)} %pad_maximum_fusion.refs_3_), channel_id=1, source_target_pairs={{0,4},{1,5},{2,6},{3,7},{4,0},{5,1},{6,2},{7,3},{8,12},{9,13},{10,... | collective-permute-start | bytes 2027528 | tf_op jit(solution)/shard_map/ppermute | solution.py:20
